TPU v7x, 128 devices: a whole 4x4x4 slice. The times are simulated.
128 devices in a mesh: section: 2 (over core), expert: 32 (over z, x, y_hi), dp: 2 (over y_lo).
Axes of the slice: x: 4, y: 4 (y_hi: 2, y_lo: 2; y = y_hi * 2 + y_lo), z: 4, core: 2. Of those that a mesh axis runs over, the one named last changes fastest.
Arguments:
- images_in: bfloat16 [2, 64, 197, 384], P(None, ('expert', 'dp')), may hold values from -6 to 6
- cotangent: bfloat16 [2, 64, 197, 384], P(None, ('expert', 'dp')), may hold values from -6 to 6
- gain_one: float32 [2, 384], P('section'), may hold values from 0.1 to 1.9
- w_qkv: bfloat16 [2, 384, 1152], P('section'), may hold values from -0.3125 to 0.3125
- w_out: bfloat16 [2, 384, 384], P('section'), may hold values from -1.75 to 1.75
- gain_two: float32 [2, 384], P('section'), may hold values from 0.1 to 1.9
- w_router: float32 [2, 384, 32], P('section'), may hold values from -0.21875 to 0.21875
- w_in: bfloat16 [2, 32, 384, 1536], P('section', 'expert'), may hold values from -0.3125 to 0.3125
- w_back: bfloat16 [2, 32, 1536, 384], P('section', 'expert'), may hold values from -2 to 2
- routes: int32 [2, 2, 64, 197, 2], P('section', None, ('expert', 'dp')), may hold values from 0 to 31, all different within a row; in each aligned block of 197 rows (0 to 196, 197 to 393, ..., all dimensions but the last counted through in order) at most 19 rows name the same one
- keep: int32 [2, 2, 64, 197, 2], P('section', None, ('expert', 'dp')), may hold values 0 or 1
Outputs:
- activations: bfloat16 [2, 2, 64, 197, 384], P('section', None, ('expert', 'dp'))
- input_grad: float32 [2, 2, 64, 197, 384], P('section', None, ('expert', 'dp'))
- d_gain_one: float32 [2, 384], P('section')
- d_w_qkv: float32 [2, 384, 1152], P('section')
- d_w_out: float32 [2, 384, 384], P('section')
- d_gain_two: float32 [2, 384], P('section')
- d_w_router: float32 [2, 384, 32], P('section')
- d_w_in: float32 [2, 32, 384, 1536], P('section', 'expert')
- d_w_back: float32 [2, 32, 1536, 384], P('section', 'expert')
Inputs may be any that keep to these rules, and one draw needn't show every extreme that they name: `routes`: A token's two choices are different experts. In the tokens of one device for one block and micro-batch (1 images), no expert is chosen more than 19 times.
All inputs are finite; a program needn't handle non-finite values. No bound on the sum of `keep` on one device may be relied on, other than what follows from the above.
Results may differ from a plain program's by a relative error of at most 0.02.
Values may be sent and summed in bfloat16 or wider, within the bound.
A program may use at most 128 MiB of HBM per device.

v0:
```python
from functools import partial

import jax
import jax.numpy as jnp
from jax import lax
from jax.sharding import PartitionSpec as P

HEADS = 6
HEAD = 64


EPSILON = 1e-06
HIGHEST = lax.Precision.HIGHEST


def passed_along(value, axis, steps):
    count = lax.axis_size(axis)
    leading, last = (max(0, -steps), min(count, count - steps))
    return lax.ppermute(value, axis, [(source, source + steps) for source in range(leading, last)])


def layer_norm(values, gain):
    center = values - jnp.mean(values, axis=-1, keepdims=True)
    spread = jnp.mean(center * center, axis=-1, keepdims=True)
    return center * lax.rsqrt(spread + EPSILON) * gain


def norm_route(mixed, gain_two, w_router):
    second = layer_norm(mixed, gain_two)
    logits = jnp.dot(second, w_router, precision=HIGHEST)
    return (second, jax.nn.softmax(logits, axis=-1))


def exact_gelu(values):
    return jax.nn.gelu(values, approximate=False)


def split_heads(qkv):
    images, seq = (qkv.shape[0], qkv.shape[1])
    parts = qkv.reshape(images, seq, 3, HEADS, HEAD)
    return (parts[:, :, 0], parts[:, :, 1], parts[:, :, 2])


def attention_forward(qkv):
    images, seq = (qkv.shape[0], qkv.shape[1])
    query, keys, values = split_heads(qkv)
    scores = jnp.einsum(
        "ishd,ithd->ihst", query, keys, preferred_element_type=jnp.float32
    ) * HEAD ** (-0.5)
    top = jnp.max(scores, axis=-1, keepdims=True)
    total = top + jnp.log(jnp.sum(jnp.exp(scores - top), axis=-1, keepdims=True))
    weights = jnp.exp(scores - total).astype(jnp.bfloat16)
    result = jnp.einsum("ihst,ithd->ishd", weights, values, preferred_element_type=jnp.float32)
    return (result.reshape(images, seq, HEADS * HEAD), total)


def attention_backward(qkv, total, d_attended):
    images, seq = (qkv.shape[0], qkv.shape[1])
    query, keys, values = split_heads(qkv)
    d_heads = d_attended.reshape(images, seq, HEADS, HEAD)
    scores = jnp.einsum(
        "ishd,ithd->ihst", query, keys, preferred_element_type=jnp.float32
    ) * HEAD ** (-0.5)
    probs = jnp.exp(scores - total)
    weights = probs.astype(jnp.bfloat16)
    d_values = jnp.einsum("ihst,ishd->ithd", weights, d_heads, preferred_element_type=jnp.float32)
    d_probs = jnp.einsum("ishd,ithd->ihst", d_heads, values, preferred_element_type=jnp.float32)
    inner = jnp.sum(probs * d_probs, axis=-1, keepdims=True)
    d_scores = (probs * (d_probs - inner)).astype(jnp.bfloat16)
    d_query = jnp.einsum(
        "ihst,ithd->ishd", d_scores, keys, preferred_element_type=jnp.float32
    ) * HEAD ** (-0.5)
    d_keys = jnp.einsum(
        "ihst,ishd->ithd", d_scores, query, preferred_element_type=jnp.float32
    ) * HEAD ** (-0.5)
    return jnp.stack([d_query, d_keys, d_values], axis=2).reshape(images, seq, 3 * HEADS * HEAD)


def slot_places(pairs, experts, capacity):
    flat = pairs.reshape(-1)
    marks = (flat[:, None] == jnp.arange(experts, dtype=jnp.int32)[None, :]).astype(jnp.int32)
    before = jnp.cumsum(marks, axis=0) - marks
    return flat * capacity + jnp.sum(before * marks, axis=1)


def to_experts(arrived, local):
    sources = arrived.shape[0] // local
    capacity, width = (arrived.shape[1], arrived.shape[2])
    return (
        arrived.reshape(sources, local, capacity, width)
        .transpose(1, 0, 2, 3)
        .reshape(local, sources * capacity, width)
    )


def from_experts(rows, sources, capacity):
    local, width = (rows.shape[0], rows.shape[2])
    return (
        rows.reshape(local, sources, capacity, width)
        .transpose(1, 0, 2, 3)
        .reshape(sources * local, capacity, width)
    )


def block_forward(xin, routes, keep, weights):
    gain_one, w_qkv, w_out, gain_two, w_router, w_in, w_back = weights
    images, seq, width = xin.shape
    experts = w_router.shape[1]
    local = w_in.shape[0]
    capacity = max(2, 3 * images * seq // experts + 1)
    normed = layer_norm(xin, gain_one).astype(jnp.bfloat16)
    qkv = jnp.einsum("isd,de->ise", normed, w_qkv, preferred_element_type=jnp.float32).astype(
        jnp.bfloat16
    )
    attended, total = attention_forward(qkv)
    attended = attended.astype(jnp.bfloat16)
    mixed = xin + jnp.einsum("isd,de->ise", attended, w_out, preferred_element_type=jnp.float32)
    mixed = mixed.reshape(images * seq, width)
    second, probs = norm_route(mixed, gain_two, w_router)
    pairs = routes.reshape(-1, 2)
    place = slot_places(pairs, experts, capacity)
    marks = (pairs[:, :, None] == jnp.arange(experts, dtype=jnp.int32)).astype(jnp.float32)
    marks = marks * keep.reshape(-1, 2, 1).astype(jnp.float32)
    gates = jnp.sum(marks * probs[:, None, :], axis=2)
    filled = jnp.zeros((experts * capacity, width), jnp.bfloat16)
    filled = filled.at[place].set(jnp.repeat(second.astype(jnp.bfloat16), 2, axis=0))
    arrived = lax.all_to_all(
        filled.reshape(experts, capacity, width), "expert", split_axis=0, concat_axis=0, tiled=True
    )
    inputs = to_experts(arrived, local)
    hidden = jnp.einsum("erd,edf->erf", inputs, w_in, preferred_element_type=jnp.float32)
    active = exact_gelu(hidden).astype(jnp.bfloat16)
    produced = jnp.einsum(
        "erf,efd->erd", active, w_back, preferred_element_type=jnp.float32
    ).astype(jnp.bfloat16)
    returned = lax.all_to_all(
        from_experts(produced, arrived.shape[0] // local, capacity),
        "expert",
        split_axis=0,
        concat_axis=0,
        tiled=True,
    )
    picked = (
        returned.reshape(experts * capacity, width)[place].astype(jnp.float32).reshape(-1, 2, width)
    )
    result = mixed + jnp.sum(gates[:, :, None] * picked, axis=1)
    saved = (xin, qkv, total, attended, mixed, place, picked, inputs, hidden, active)
    return (result.reshape(images, seq, width), saved)


def block_backward(grad, saved, routes, keep, weights):
    gain_one, w_qkv, w_out, gain_two, w_router, w_in, w_back = weights
    xin, qkv, total, attended, mixed, place, picked, inputs, hidden, active = saved
    images, seq, width = xin.shape
    experts = w_router.shape[1]
    local = w_in.shape[0]
    sources = experts // local
    capacity = inputs.shape[1] // sources
    grad_rows = grad.reshape(images * seq, width)
    route_out, route_pull = jax.vjp(norm_route, mixed, gain_two, w_router)
    probs = route_out[1]
    pairs = routes.reshape(-1, 2)
    marks = (pairs[:, :, None] == jnp.arange(experts, dtype=jnp.int32)).astype(jnp.float32)
    marks = marks * keep.reshape(-1, 2, 1).astype(jnp.float32)
    gates = jnp.sum(marks * probs[:, None, :], axis=2)
    d_gates = jnp.sum(picked * grad_rows[:, None, :], axis=2)
    d_probs = jnp.sum(marks * d_gates[:, :, None], axis=1)
    d_picked = (gates[:, :, None] * grad_rows[:, None, :]).reshape(-1, width)
    d_returned = (
        jnp.zeros((experts * capacity, width), jnp.float32)
        .at[place]
        .set(d_picked)
        .astype(jnp.bfloat16)
    )
    backward_rows = lax.all_to_all(
        d_returned.reshape(experts, capacity, width),
        "expert",
        split_axis=0,
        concat_axis=0,
        tiled=True,
    )
    d_produced = to_experts(backward_rows, local)
    d_active = jnp.einsum("erd,efd->erf", d_produced, w_back, preferred_element_type=jnp.float32)
    gelu_pull = jax.vjp(exact_gelu, hidden)[1]
    d_hidden = gelu_pull(d_active)[0].astype(jnp.bfloat16)
    d_inputs = jnp.einsum(
        "erf,edf->erd", d_hidden, w_in, preferred_element_type=jnp.float32
    ).astype(jnp.bfloat16)
    d_filled = lax.all_to_all(
        from_experts(d_inputs, sources, capacity), "expert", split_axis=0, concat_axis=0, tiled=True
    )
    d_picked_rows = d_filled.reshape(experts * capacity, width)[place].astype(jnp.float32)
    d_second = jnp.sum(d_picked_rows.reshape(-1, 2, width), axis=1)
    d_mixed_norm, d_gain_two, d_router = route_pull((d_second, d_probs))
    d_mixed = grad_rows + d_mixed_norm
    d_branch = d_mixed.astype(jnp.bfloat16)
    flat_attended = attended.reshape(images * seq, width)
    d_w_out = jnp.einsum("nd,ne->de", flat_attended, d_branch, preferred_element_type=jnp.float32)
    d_attended = jnp.einsum("ne,de->nd", d_branch, w_out, preferred_element_type=jnp.float32)
    d_attended = d_attended.astype(jnp.bfloat16).reshape(images, seq, width)
    d_qkv = attention_backward(qkv, total, d_attended).astype(jnp.bfloat16)
    normed, norm_pull = jax.vjp(layer_norm, xin, gain_one)
    normed_low = normed.astype(jnp.bfloat16)
    d_w_qkv = jnp.einsum("isd,ise->de", normed_low, d_qkv, preferred_element_type=jnp.float32)
    d_normed = jnp.einsum("ise,de->isd", d_qkv, w_qkv, preferred_element_type=jnp.float32)
    d_input_norm, d_gain_one = norm_pull(d_normed)
    d_xin = d_mixed.reshape(images, seq, width) + d_input_norm
    dense = (d_gain_one, d_w_qkv, d_w_out, d_gain_two, d_router)
    rows = (inputs, d_hidden, active, d_produced)
    return (d_xin, dense, rows)


def expert_weight_grads(rows):
    inputs, d_hidden, active, d_produced = rows
    d_first = jnp.einsum("erd,erf->edf", inputs, d_hidden, preferred_element_type=jnp.float32)
    d_second = jnp.einsum("erf,erd->efd", active, d_produced, preferred_element_type=jnp.float32)
    return (d_first, d_second)


def body(
    images_in, cotangent, gain_one, w_qkv, w_out, gain_two, w_router, w_in, w_back, routes, keep
):
    section = lax.axis_index("section")
    first = section == 0
    micro = images_in.shape[0]
    weights = (gain_one[0], w_qkv[0], w_out[0], gain_two[0], w_router[0], w_in[0], w_back[0])
    blank = jnp.zeros(images_in.shape[1:], jnp.bfloat16)
    received = blank
    outputs = [blank] * micro
    stored = [None] * micro
    for tick in range(micro + 1):
        index = jnp.clip(tick - section, 0, micro - 1)
        xin = jnp.where(first, images_in[min(tick, micro - 1)], received).astype(jnp.float32)
        tick_routes = lax.dynamic_index_in_dim(routes[0], index, 0, keepdims=False)
        tick_keep = lax.dynamic_index_in_dim(keep[0], index, 0, keepdims=False)
        result, saved = block_forward(xin, tick_routes, tick_keep, weights)
        low_out = result.astype(jnp.bfloat16)
        for number in range(max(tick - 1, 0), min(tick, micro - 1) + 1):
            hit = tick - section == number
            outputs[number] = jnp.where(hit, low_out, outputs[number])
            if stored[number] is None:
                stored[number] = saved
            else:
                stored[number] = jax.tree.map(partial(jnp.where, hit), saved, stored[number])
        if tick < micro:
            received = passed_along(low_out, "section", 1)
    incoming = blank
    input_grads = [jnp.zeros(images_in.shape[1:], jnp.float32)] * micro
    dense_total = None
    expert_total = None
    for tick in range(micro + 1):
        raw = tick + section - 1
        index = jnp.clip(raw, 0, micro - 1)
        valid = (raw >= 0) & (raw < micro)
        grad = jnp.where(first, incoming, cotangent[min(tick, micro - 1)]).astype(jnp.float32)
        tick_routes = lax.dynamic_index_in_dim(routes[0], index, 0, keepdims=False)
        tick_keep = lax.dynamic_index_in_dim(keep[0], index, 0, keepdims=False)
        chosen = jax.tree.map(
            partial(jnp.where, first), stored[max(tick - 1, 0)], stored[min(tick, micro - 1)]
        )
        saved = chosen
        d_xin, dense, rows = block_backward(grad, saved, tick_routes, tick_keep, weights)
        dense = jax.tree.map(lambda value: jnp.where(valid, value, 0.0), dense)
        if dense_total is None:
            dense_total = dense
        else:
            dense_total = jax.tree.map(jnp.add, dense_total, dense)
        pair = jax.tree.map(lambda value: jnp.where(valid, value, 0.0), expert_weight_grads(rows))
        if expert_total is None:
            expert_total = pair
        else:
            expert_total = jax.tree.map(jnp.add, expert_total, pair)
        d_low = d_xin.astype(jnp.bfloat16)
        value = jnp.where(first, d_xin, d_low.astype(jnp.float32))
        for number in range(max(tick - 1, 0), min(tick, micro - 1) + 1):
            input_grads[number] = jnp.where(raw == number, value, input_grads[number])
        if tick < micro:
            incoming = passed_along(d_low, "section", -1)
    d_gain_one, d_w_qkv, d_w_out, d_gain_two, d_router = lax.psum(
        (dense_total[0], dense_total[1], dense_total[2], dense_total[3], dense_total[4]),
        ("expert", "dp"),
    )
    d_first, d_second = (
        lax.psum(expert_total[0].astype(jnp.bfloat16), "dp").astype(jnp.float32),
        lax.psum(expert_total[1].astype(jnp.bfloat16), "dp").astype(jnp.float32),
    )
    return (
        jnp.stack(outputs)[None],
        jnp.stack(input_grads)[None],
        d_gain_one[None],
        d_w_qkv[None],
        d_w_out[None],
        d_gain_two[None],
        d_router[None],
        d_first[None],
        d_second[None],
    )


def solution(mesh):
    return jax.shard_map(
        body,
        mesh=mesh,
        in_specs=(
            P(None, ("expert", "dp"), None, None),
            P(None, ("expert", "dp"), None, None),
            P("section", None),
            P("section", None, None),
            P("section", None, None),
            P("section", None),
            P("section", None, None),
            P("section", "expert", None, None),
            P("section", "expert", None, None),
            P("section", None, ("expert", "dp"), None, None),
            P("section", None, ("expert", "dp"), None, None),
        ),
        out_specs=(
            P("section", None, ("expert", "dp"), None, None),
            P("section", None, ("expert", "dp"), None, None),
            P("section", None),
            P("section", None, None),
            P("section", None, None),
            P("section", None),
            P("section", None, None),
            P("section", "expert", None, None),
            P("section", "expert", None, None),
        ),
        check_vma=False,
    )
```

profile of v0, /device:TPU:0, one launch (start us, length us, event | category | flops | bytes accessed | tf_op | source)
XLA Modules:
  0.0 932.5 jit_solution(11202966981415552260)
XLA Ops:
  7.2 2.4 fusion.372
  29.0 10.9 %all-to-all-start = ((bf16[32,19,384]{2,1,0:T(8,128)(2,1)}), bf16[32,19,384]{2,1,0:T(8,128)(2,1)S(1)}, u32[]{:S(2)}, u32[]{:S(2)}) async-start(bf16[32,19,384]{2,1,0:T(8,128)(2,1)} %reshape.2389), calls=%async_computation | async-start | bytes 1179648 | tf_op jit(solution)/shard_map/all_to_all | solution.py:127
  44.4 10.0 %all-to-all-done = bf16[32,19,384]{2,1,0:T(8,128)(2,1)S(1)} async-done(((bf16[32,19,384]{2,1,0:T(8,128)(2,1)}), bf16[32,19,384]{2,1,0:T(8,128)(2,1)S(1)}, u32[]{:S(2)}, u32[]{:S(2)}) %all-to-all-start) | async-done | bytes 466976 | tf_op jit(solution)/shard_map/all_to_all | solution.py:127
  54.5 10.0 %fusion.2 = (bf16[608,1536]{1,0:T(8,128)(2,1)S(1)}, f32[608,1536]{1,0:T(8,128)}) fusion(bf16[608,384]{1,0:T(8,128)(2,1)S(1)} %reshape.2390, bf16[1,1,384,1536]{3,2,1,0:T(8,128)(2,1)S(1)} %copy-done), kind=kOutput, calls=%fused_computation.20 | convolution fusion | flops 777928704 | bytes 7249920 | tf_op jit(solution)/shard_map/erd,edf->erf/dot_general | solution.py:131
  67.9 4.1 all-to-all-start.1
  73.9 11.4 %all-to-all-done.1 = bf16[32,19,384]{2,1,0:T(8,128)(2,1)S(1)} async-done(((bf16[32,19,384]{2,1,0:T(8,128)(2,1)}), bf16[32,19,384]{2,1,0:T(8,128)(2,1)S(1)}, u32[]{:S(2)}, u32[]{:S(2)}) %all-to-all-start.1) | async-done | bytes 466976 | tf_op jit(solution)/shard_map/all_to_all | solution.py:136
  85.5 2.5 gather_fusion
  95.5 2.3 mul.1218
  100.3 2.5 broadcast_select_fusion.15
  113.3 3.1 scatter_custom_fusion.1
  118.4 5.0 all-to-all-start.2
  126.8 9.3 all-to-all-done.2
  138.1 11.1 %fusion.5 = (bf16[608,1536]{1,0:T(8,128)(2,1)S(1)}, f32[608,1536]{1,0:T(8,128)}) fusion(bf16[608,384]{1,0:T(8,128)(2,1)} %reshape.2404, bf16[1,1,384,1536]{3,2,1,0:T(8,128)(2,1)S(1)} %copy-done), kind=kOutput, calls=%fused_computation.23 | convolution fusion | flops 777928704 | bytes 7249920 | tf_op jit(solution)/shard_map/erd,edf->erf/dot_general | solution.py:131
  154.4 4.6 all-to-all-start.3
  162.8 8.9 all-to-all-done.3
  172.9 2.7 gather_fusion.1
  177.7 3.2 multiply_reduce_fusion.5
  190.6 3.4 scatter_custom_fusion.3
  198.1 4.8 all-to-all-start.6
  209.5 6.0 all-to-all-done.6
  217.6 10.9 %fusion.13 = bf16[608,1536]{1,0:T(8,128)(2,1)S(1)} fusion(bf16[608,384]{1,0:T(8,128)(2,1)} %reshape.2419, f32[608,1536]{1,0:T(8,128)} %get-tuple-element.170, f32[608,1536]{1,0:T(8,128)} %get-tuple-element.162, pred[]{:T(512)S(6)} %eq.181, bf16[1,1,1536,384]{3,2,1,0:T(8,128)(2,1)} %param.19), kind=kOutput, calls=%fused_computation.31 | convolution fusion | flops 785399808 | bytes 10985473 | tf_op jit(solution)/shard_map/erd,efd->erf/dot_general | solution.py:183
  233.7 4.8 all-to-all-start.7
  241.5 9.7 %all-to-all-done.7 = bf16[32,19,384]{2,1,0:T(8,128)(2,1)} async-done(((bf16[32,19,384]{2,1,0:T(8,128)(2,1)}), bf16[32,19,384]{2,1,0:T(8,128)(2,1)}, u32[]{:S(2)}, u32[]{:S(2)}) %all-to-all-start.7) | async-done | bytes 466976 | tf_op jit(solution)/shard_map/all_to_all | solution.py:189
  252.5 2.5 gather_fusion.3
  257.2 2.5 reduce_sum.832
  259.7 2.4 multiply_reduce_fusion.11
  291.9 3.1 scatter_custom_fusion.2
  297.0 5.0 all-to-all-start.4
  309.9 7.2 all-to-all-done.4
  318.3 10.0 %fusion.8 = (bf16[608,1536]{1,0:T(8,128)(2,1)S(1)}, f32[608,1536]{1,0:T(8,128)}) fusion(bf16[608,384]{1,0:T(8,128)(2,1)S(1)} %reshape.2416, bf16[1,1,384,1536]{3,2,1,0:T(8,128)(2,1)S(1)} %copy-done), kind=kOutput, calls=%fused_computation.26 | convolution fusion | flops 777928704 | bytes 7249920 | tf_op jit(solution)/shard_map/erd,edf->erf/dot_general | solution.py:131
  333.5 4.6 all-to-all-start.5
  340.7 2.3 mul.1275
  343.0 10.6 %all-to-all-done.5 = bf16[32,19,384]{2,1,0:T(8,128)(2,1)} async-done(((bf16[32,19,384]{2,1,0:T(8,128)(2,1)}), bf16[32,19,384]{2,1,0:T(8,128)(2,1)}, u32[]{:S(2)}, u32[]{:S(2)}) %all-to-all-start.5) | async-done | bytes 466976 | tf_op jit(solution)/shard_map/all_to_all | solution.py:136
  354.8 2.5 gather_fusion.2
  358.7 2.8 multiply_reduce_fusion.4
  366.4 3.4 scatter_custom_fusion.4
  373.9 4.6 all-to-all-start.8
  387.6 2.4 broadcast_select_fusion.11
  397.6 12.3 %fusion.18 = bf16[608,1536]{1,0:T(8,128)(2,1)S(1)} fusion(bf16[608,384]{1,0:T(8,128)(2,1)S(1)} %reshape.2430, pred[]{:T(512)S(6)} %eq.182, f32[608,1536]{1,0:T(8,128)} %get-tuple-element.170, f32[608,1536]{1,0:T(8,128)} %get-tuple-element.162, pred[]{:T(512)S(6)} %eq.181, f32[608,1536]{1,0:T(8,128)} %get-tuple-element.186, pred[]{:T(512)S(6)} %eq.206, ...), kind=kOutput, calls=%fused_computation.36 | convolution fusion | flops 787267584 | bytes 14721027 | tf_op jit(solution)/shard_map/erd,efd->erf/dot_general | solution.py:183
  415.1 10.0 %all-to-all-start.9 = ((bf16[32,19,384]{2,1,0:T(8,128)(2,1)}), bf16[32,19,384]{2,1,0:T(8,128)(2,1)}, u32[]{:S(2)}, u32[]{:S(2)}) async-start(bf16[32,19,384]{2,1,0:T(8,128)(2,1)} %reshape_transpose_reshape.28), calls=%async_computation.9 | async-start | bytes 1179648 | tf_op jit(solution)/shard_map/all_to_all | solution.py:189
  425.1 3.7 convolution_select_fusion.4
  428.9 2.8 fusion.70
  431.7 7.0 all-to-all-done.9
  440.0 2.5 gather_fusion.4
  442.5 2.2 reshape.2465
  444.7 2.5 reduce_sum.847
  447.2 2.4 multiply_reduce_fusion.10
  463.2 2.5 convolution_select_fusion.7
  476.4 3.1 scatter_custom_fusion.5
  481.7 4.6 all-to-all-start.10
  486.4 5.0 fusion.68
  493.8 8.2 all-to-all-done.10
  504.0 11.6 %fusion.23 = bf16[608,1536]{1,0:T(8,128)(2,1)S(1)} fusion(bf16[608,384]{1,0:T(8,128)(2,1)S(1)} %reshape.2441, f32[608,1536]{1,0:T(8,128)} %get-tuple-element.186, f32[608,1536]{1,0:T(8,128)} %get-tuple-element.170, pred[]{:T(512)S(6)} %eq.206, bf16[1,1,1536,384]{3,2,1,0:T(8,128)(2,1)} %param.19), kind=kOutput, calls=%fused_computation.41 | convolution fusion | flops 785399808 | bytes 10985473 | tf_op jit(solution)/shard_map/erd,efd->erf/dot_general | solution.py:183
  520.8 4.6 all-to-all-start.11
  525.7 4.5 fusion.75
  530.3 2.4 fusion.76
  532.7 7.6 all-to-all-done.11
  541.6 2.5 gather_fusion.5
  544.1 2.2 reshape.2468
  546.4 2.5 reduce_sum.862
  548.9 2.4 multiply_reduce_fusion.9
  573.4 343.6 %all-reduce.3 = (f32[1,384]{1,0:T(1,128)}, f32[1,384]{1,0:T(1,128)}, f32[1,384,32]{1,2,0:T(8,128)}) all-reduce(f32[1,384]{1,0:T(1,128)S(1)} %broadcast_in_dim.248, f32[1,384]{1,0:T(1,128)S(1)} %broadcast_in_dim.253, f32[1,384,32]{1,2,0:T(8,128)S(1)} %fusion.121), channel_id=1, replica_groups=mesh['section'=2,'expert'=32,'dp'=2] {'expert','dp'}, use_global_device_ids=true, to_apply=%region_96.97 | all-reduce | flops 13056 | bytes 104448 | tf_op jit(solution)/shard_map/psum | solution.py:279
  917.0 3.1 broadcast_in_dim.258
  921.6 2.9 copy.285
  (655 shorter events, 246.9 us)
Async XLA Ops:
  7.2 47.3 %copy-start = (bf16[1,1,384,1536]{3,2,1,0:T(8,128)(2,1)S(1)}, bf16[1,1,384,1536]{3,2,1,0:T(8,128)(2,1)}, u32[]{:S(2)}) copy-start(bf16[1,1,384,1536]{3,2,1,0:T(8,128)(2,1)} %param.18) | copy-start | bytes 3538948
  13.1 9.4 %copy-start.5 = (bf16[1,384,384]{2,1,0:T(8,128)(2,1)S(1)}, bf16[1,384,384]{2,1,0:T(8,128)(2,1)}, u32[]{:S(2)}) copy-start(bf16[1,384,384]{2,1,0:T(8,128)(2,1)} %param.15) | copy-start | bytes 884740
  17.4 23.1 %copy-start.46 = (f32[1,384,32]{1,2,0:T(8,128)S(1)}, f32[1,384,32]{1,2,0:T(8,128)}, u32[]{:S(2)}) copy-start(f32[1,384,32]{1,2,0:T(8,128)} %param.17) | copy-start | bytes 147460
  18.1 23.1 %copy-start.92 = (s32[1,2,1,197,2]{3,4,2,1,0:T(2,128)S(1)}, s32[1,2,1,197,2]{3,4,2,1,0:T(2,128)}, u32[]{:S(2)}) copy-start(s32[1,2,1,197,2]{3,4,2,1,0:T(2,128)} %param.21) | copy-start | bytes 9460
  25.4 19.0 %copy-start.153 = (s32[394,1]{0,1:T(1,128)}, s32[394,1]{0,1:T(1,128)S(1)}, u32[]{:S(2)}) copy-start(s32[394,1]{0,1:T(1,128)S(1)} %get-tuple-element.154) | copy-start | bytes 4732
  25.4 19.0 %copy-start.154 = (s32[394,1]{0,1:T(1,128)}, s32[394,1]{0,1:T(1,128)S(1)}, u32[]{:S(2)}) copy-start(s32[394,1]{0,1:T(1,128)S(1)} %get-tuple-element.155) | copy-start | bytes 4732
  29.0 25.3 %all-to-all-start = ((bf16[32,19,384]{2,1,0:T(8,128)(2,1)}), bf16[32,19,384]{2,1,0:T(8,128)(2,1)S(1)}, u32[]{:S(2)}, u32[]{:S(2)}) async-start(bf16[32,19,384]{2,1,0:T(8,128)(2,1)} %reshape.2389), calls=%async_computation | async-start | bytes 1179648 | tf_op jit(solution)/shard_map/all_to_all | solution.py:127
  43.2 21.4 %copy-start.156 = (s32[394,1]{0,1:T(1,128)}, s32[394,1]{0,1:T(1,128)S(1)}, u32[]{:S(2)}) copy-start(s32[394,1]{0,1:T(1,128)S(1)} %compare_select_fusion.2) | copy-start | bytes 4732
  54.3 10.2 %copy-start.28 = (bf16[32,19,384]{2,1,0:T(8,128)(2,1)}, bf16[32,19,384]{2,1,0:T(8,128)(2,1)S(1)}, u32[]{:S(2)}) copy-start(bf16[32,19,384]{2,1,0:T(8,128)(2,1)S(1)} %all-to-all-done) | copy-start | bytes 1400836
  54.5 11.3 %copy-start.164 = (bf16[1,1,1536,384]{3,2,1,0:T(8,128)(2,1)S(1)}, bf16[1,1,1536,384]{3,2,1,0:T(8,128)(2,1)}, u32[]{:S(2)}) copy-start(bf16[1,1,1536,384]{3,2,1,0:T(8,128)(2,1)} %param.19) | copy-start | bytes 3538948
  66.9 18.6 %copy-start.145 = (s32[1024]{0:T(1024)S(1)}, s32[1024]{0:T(1024)}, u32[]{:S(2)}) copy-start(s32[1024]{0:T(1024)} %pad_clamp_fusion.5) | copy-start | bytes 12292
  67.9 17.4 %all-to-all-start.1 = ((bf16[32,19,384]{2,1,0:T(8,128)(2,1)}), bf16[32,19,384]{2,1,0:T(8,128)(2,1)S(1)}, u32[]{:S(2)}, u32[]{:S(2)}) async-start(bf16[32,19,384]{2,1,0:T(8,128)(2,1)} %reshape_transpose_reshape.24), calls=%async_computation.1 | async-start | bytes 1179648 | tf_op jit(solution)/shard_map/all_to_all | solution.py:136
  73.2 20.7 %copy-start.152 = (s32[394,1]{0,1:T(1,128)S(1)}, s32[394,1]{0,1:T(1,128)}, u32[]{:S(2)}) copy-start(s32[394,1]{0,1:T(1,128)} %get-tuple-element.110) | copy-start | bytes 4732
  73.9 23.9 %copy-start.51 = (f32[197,384]{1,0:T(8,128)}, f32[197,384]{1,0:T(8,128)S(1)}, u32[]{:S(2)}) copy-start(f32[197,384]{1,0:T(8,128)S(1)} %fusion.246) | copy-start | bytes 907780
  85.5 12.3 %copy-start.151 = (s32[394,1]{0,1:T(1,128)S(1)}, s32[394,1]{0,1:T(1,128)}, u32[]{:S(2)}) copy-start(s32[394,1]{0,1:T(1,128)} %get-tuple-element.92) | copy-start | bytes 4732
  85.5 14.7 %copy-start.1 = (bf16[1,384,1152]{2,1,0:T(8,128)(2,1)S(1)}, bf16[1,384,1152]{2,1,0:T(8,128)(2,1)}, u32[]{:S(2)}) copy-start(bf16[1,384,1152]{2,1,0:T(8,128)(2,1)} %param.14) | copy-start | bytes 2654212
  91.9 6.5 collective-permute-start
  108.3 17.3 %copy-start.118 = (s32[1,1,1,197,2]{3,4,2,1,0:T(2,128)S(1)}, s32[1,1,1,197,2]{3,4,2,1,0:T(2,128)}, u32[]{:S(2)}) copy-start(s32[1,1,1,197,2]{3,4,2,1,0:T(2,128)} %copy-done.117) | copy-start | bytes 4732
  108.3 17.3 %copy-start.155 = (f32[197,2]{0,1:T(2,128)S(1)}, f32[197,2]{0,1:T(2,128)}, u32[]{:S(2)}) copy-start(f32[197,2]{0,1:T(2,128)} %get-tuple-element.151) | copy-start | bytes 4732
  109.7 39.5 %copy-start.2 = (f32[197,384]{1,0:T(8,128)}, f32[197,384]{1,0:T(8,128)S(1)}, u32[]{:S(2)}) copy-start(f32[197,384]{1,0:T(8,128)S(1)} %get-tuple-element.121) | copy-start | bytes 907780
  118.4 17.7 %all-to-all-start.2 = ((bf16[32,19,384]{2,1,0:T(8,128)(2,1)}), bf16[32,19,384]{2,1,0:T(8,128)(2,1)}, u32[]{:S(2)}, u32[]{:S(2)}) async-start(bf16[32,19,384]{2,1,0:T(8,128)(2,1)} %reshape.2403), calls=%async_computation.2 | async-start | bytes 1179648 | tf_op jit(solution)/shard_map/all_to_all | solution.py:127
  125.4 78.3 %copy-start.94 = (f32[197]{0:T(256)}, f32[197]{0:T(256)S(1)}, u32[]{:S(2)}) copy-start(f32[197]{0:T(256)S(1)} %broadcast_multiply_fusion.8) | copy-start | bytes 2368
  126.2 23.0 %copy-start.108 = (f32[197]{0:T(256)}, f32[197]{0:T(256)S(1)}, u32[]{:S(2)}) copy-start(f32[197]{0:T(256)S(1)} %fusion.353) | copy-start | bytes 2368
  126.8 76.8 %copy-start.95 = (f32[197]{0:T(256)}, f32[197]{0:T(256)S(1)}, u32[]{:S(2)}) copy-start(f32[197]{0:T(256)S(1)} %get-tuple-element.173) | copy-start | bytes 2368
  138.1 12.4 %copy-start.165 = (bf16[1,1,1536,384]{3,2,1,0:T(8,128)(2,1)S(1)}, bf16[1,1,1536,384]{3,2,1,0:T(8,128)(2,1)}, u32[]{:S(2)}) copy-start(bf16[1,1,1536,384]{3,2,1,0:T(8,128)(2,1)} %param.19) | copy-start | bytes 3538948
  150.5 10.0 %copy-start.42 = (bf16[197,1152]{1,0:T(8,128)(2,1)S(1)}, bf16[197,1152]{1,0:T(8,128)(2,1)}, u32[]{:S(2)}) copy-start(bf16[197,1152]{1,0:T(8,128)(2,1)} %get-tuple-element.176) | copy-start | bytes 1361668
  154.4 17.3 %all-to-all-start.3 = ((bf16[32,19,384]{2,1,0:T(8,128)(2,1)}), bf16[32,19,384]{2,1,0:T(8,128)(2,1)}, u32[]{:S(2)}, u32[]{:S(2)}) async-start(bf16[32,19,384]{2,1,0:T(8,128)(2,1)} %reshape_transpose_reshape.25), calls=%async_computation.3 | async-start | bytes 1179648 | tf_op jit(solution)/shard_map/all_to_all | solution.py:136
  181.0 22.7 %copy-start.3 = (f32[197,384]{1,0:T(8,128)S(1)}, f32[197,384]{1,0:T(8,128)}, u32[]{:S(2)}) copy-start(f32[197,384]{1,0:T(8,128)} %copy-done.2) | copy-start | bytes 907780
  181.0 22.7 %copy-start.109 = (f32[197]{0:T(256)S(1)}, f32[197]{0:T(256)}, u32[]{:S(2)}) copy-start(f32[197]{0:T(256)} %copy-done.108) | copy-start | bytes 2368
  182.7 22.9 %copy-start.78 = (bf16[1,197,384]{2,1,0:T(8,128)(2,1)}, bf16[1,197,384]{2,1,0:T(8,128)(2,1)S(1)}, u32[]{:S(2)}) copy-start(bf16[1,197,384]{2,1,0:T(8,128)(2,1)S(1)} %get-tuple-element.95) | copy-start | bytes 453892
  182.7 22.9 %collective-permute-start.1 = (bf16[1,197,384]{2,1,0:T(8,128)(2,1)S(1)}, bf16[1,197,384]{2,1,0:T(8,128)(2,1)}, u32[]{:S(2)}, u32[]{:S(2)}) collective-permute-start(bf16[1,197,384]{2,1,0:T(8,128)(2,1)S(1)} %get-tuple-element.95), channel_id=1, source_target_pairs={{0,64},{1,65},{2,66},{3,67},{4,68},{5,69},{6,70},{7,71},{8,72},{9,... | collective-permute-start | bytes 453896 | tf_op jit(solution)/shard_map/ppermute | solution.py:19
  198.1 17.5 %all-to-all-start.6 = ((bf16[32,19,384]{2,1,0:T(8,128)(2,1)}), bf16[32,19,384]{2,1,0:T(8,128)(2,1)}, u32[]{:S(2)}, u32[]{:S(2)}) async-start(bf16[32,19,384]{2,1,0:T(8,128)(2,1)} %reshape.2418), calls=%async_computation.6 | async-start | bytes 1179648 | tf_op jit(solution)/shard_map/all_to_all | solution.py:175
  206.7 21.8 %copy-start.14 = (f32[1,197,384]{2,1,0:T(8,128)}, f32[1,197,384]{2,1,0:T(8,128)S(1)}, u32[]{:S(2)}) copy-start(f32[1,197,384]{2,1,0:T(8,128)S(1)} %get-tuple-element.99) | copy-start | bytes 907780
  206.7 21.8 %copy-start.24 = (bf16[1,197,384]{2,1,0:T(8,128)(2,1)}, bf16[1,197,384]{2,1,0:T(8,128)(2,1)S(1)}, u32[]{:S(2)}) copy-start(bf16[1,197,384]{2,1,0:T(8,128)(2,1)S(1)} %get-tuple-element.100) | copy-start | bytes 453892
  206.7 21.8 %copy-start.100 = (f32[197]{0:T(256)}, f32[197]{0:T(256)S(1)}, u32[]{:S(2)}) copy-start(f32[197]{0:T(256)S(1)} %broadcast_multiply_fusion.5) | copy-start | bytes 2368
  208.3 32.7 %copy-start.134 = (f32[197]{0:T(256)}, f32[197]{0:T(256)S(1)}, u32[]{:S(2)}) copy-start(f32[197]{0:T(256)S(1)} %get-tuple-element.203) | copy-start | bytes 2368
  229.8 22.7 %copy-start.144 = (s32[1024]{0:T(1024)S(1)}, s32[1024]{0:T(1024)}, u32[]{:S(2)}) copy-start(s32[1024]{0:T(1024)} %pad_clamp_fusion.2) | copy-start | bytes 12292
  233.7 17.5 %all-to-all-start.7 = ((bf16[32,19,384]{2,1,0:T(8,128)(2,1)}), bf16[32,19,384]{2,1,0:T(8,128)(2,1)}, u32[]{:S(2)}, u32[]{:S(2)}) async-start(bf16[32,19,384]{2,1,0:T(8,128)(2,1)} %reshape_transpose_reshape.27), calls=%async_computation.7 | async-start | bytes 1179648 | tf_op jit(solution)/shard_map/all_to_all | solution.py:189
  255.0 10.8 %copy-start.7 = (bf16[1,384,384]{2,1,0:T(8,128)(2,1)S(1)}, bf16[1,384,384]{2,1,0:T(8,128)(2,1)}, u32[]{:S(2)}) copy-start(bf16[1,384,384]{2,1,0:T(8,128)(2,1)} %param.15) | copy-start | bytes 884740
  255.0 12.5 %copy-start.89 = (f32[6,197]{1,0:T(8,128)S(1)}, f32[6,197]{1,0:T(8,128)}, u32[]{:S(2)}) copy-start(f32[6,197]{1,0:T(8,128)} %get-tuple-element.116) | copy-start | bytes 14188
  284.1 23.8 %copy-start.21 = (f32[197,384]{1,0:T(8,128)S(1)}, f32[197,384]{1,0:T(8,128)}, u32[]{:S(2)}) copy-start(f32[197,384]{1,0:T(8,128)} %copy-done.19) | copy-start | bytes 907780
  287.6 51.1 %collective-permute-start.2 = (bf16[1,197,384]{2,1,0:T(8,128)(2,1)}, bf16[1,197,384]{2,1,0:T(8,128)(2,1)}, u32[]{:S(2)}, u32[]{:S(2)}) collective-permute-start(bf16[1,197,384]{2,1,0:T(8,128)(2,1)} %fusion.325), channel_id=1, source_target_pairs={{64,0},{65,1},{66,2},{67,3},{68,4},{69,5},{70,6},{71,7},{72,8},{73... | collective-permute-start | bytes 453896 | tf_op jit(solution)/shard_map/ppermute | solution.py:19
  297.0 20.1 %all-to-all-start.4 = ((bf16[32,19,384]{2,1,0:T(8,128)(2,1)}), bf16[32,19,384]{2,1,0:T(8,128)(2,1)}, u32[]{:S(2)}, u32[]{:S(2)}) async-start(bf16[32,19,384]{2,1,0:T(8,128)(2,1)} %reshape.2415), calls=%async_computation.4 | async-start | bytes 1179648 | tf_op jit(solution)/shard_map/all_to_all | solution.py:127
  318.3 11.3 %copy-start.166 = (bf16[1,1,1536,384]{3,2,1,0:T(8,128)(2,1)S(1)}, bf16[1,1,1536,384]{3,2,1,0:T(8,128)(2,1)}, u32[]{:S(2)}) copy-start(bf16[1,1,1536,384]{3,2,1,0:T(8,128)(2,1)} %param.19) | copy-start | bytes 3538948
  331.5 23.3 %copy-start.143 = (s32[1024]{0:T(1024)S(1)}, s32[1024]{0:T(1024)}, u32[]{:S(2)}) copy-start(s32[1024]{0:T(1024)} %pad_clamp_fusion.3) | copy-start | bytes 12292
  333.5 20.1 %all-to-all-start.5 = ((bf16[32,19,384]{2,1,0:T(8,128)(2,1)}), bf16[32,19,384]{2,1,0:T(8,128)(2,1)}, u32[]{:S(2)}, u32[]{:S(2)}) async-start(bf16[32,19,384]{2,1,0:T(8,128)(2,1)} %reshape_transpose_reshape.26), calls=%async_computation.5 | async-start | bytes 1179648 | tf_op jit(solution)/shard_map/all_to_all | solution.py:136
  358.7 15.2 %copy-start.26 = (f32[197,2,384]{2,1,0:T(2,128)}, f32[197,2,384]{2,1,0:T(2,128)S(1)}, u32[]{:S(2)}) copy-start(f32[197,2,384]{2,1,0:T(2,128)S(1)} %reshape.2460) | copy-start | bytes 1815556
  358.7 19.8 %copy-start.116 = (s32[1,1,1,197,2]{3,4,2,1,0:T(2,128)S(1)}, s32[1,1,1,197,2]{3,4,2,1,0:T(2,128)}, u32[]{:S(2)}) copy-start(s32[1,1,1,197,2]{3,4,2,1,0:T(2,128)} %copy-done.115) | copy-start | bytes 4732
  373.9 22.5 %all-to-all-start.8 = ((bf16[32,19,384]{2,1,0:T(8,128)(2,1)}), bf16[32,19,384]{2,1,0:T(8,128)(2,1)}, u32[]{:S(2)}, u32[]{:S(2)}) async-start(bf16[32,19,384]{2,1,0:T(8,128)(2,1)} %reshape.2429), calls=%async_computation.8 | async-start | bytes 1179648 | tf_op jit(solution)/shard_map/all_to_all | solution.py:175
  397.6 12.3 %copy-start.86 = (bf16[608,384]{1,0:T(8,128)(2,1)}, bf16[608,384]{1,0:T(8,128)(2,1)S(1)}, u32[]{:S(2)}) copy-start(bf16[608,384]{1,0:T(8,128)(2,1)S(1)} %reshape.2430) | copy-start | bytes 1400836
  415.1 23.7 %all-to-all-start.9 = ((bf16[32,19,384]{2,1,0:T(8,128)(2,1)}), bf16[32,19,384]{2,1,0:T(8,128)(2,1)}, u32[]{:S(2)}, u32[]{:S(2)}) async-start(bf16[32,19,384]{2,1,0:T(8,128)(2,1)} %reshape_transpose_reshape.28), calls=%async_computation.9 | async-start | bytes 1179648 | tf_op jit(solution)/shard_map/all_to_all | solution.py:189
  428.9 11.1 %copy-start.142 = (s32[1024]{0:T(1024)S(1)}, s32[1024]{0:T(1024)}, u32[]{:S(2)}) copy-start(s32[1024]{0:T(1024)} %pad_clamp_fusion.1) | copy-start | bytes 12292
  431.7 15.5 %copy-start.104 = (f32[197]{0:T(256)S(1)}, f32[197]{0:T(256)}, u32[]{:S(2)}) copy-start(f32[197]{0:T(256)} %copy-done.103) | copy-start | bytes 2368
  431.7 15.5 %copy-start.111 = (f32[197]{0:T(256)S(1)}, f32[197]{0:T(256)}, u32[]{:S(2)}) copy-start(f32[197]{0:T(256)} %copy-done.110) | copy-start | bytes 2368
  431.7 17.9 %copy-start.137 = (f32[197]{0:T(256)S(1)}, f32[197]{0:T(256)}, u32[]{:S(2)}) copy-start(f32[197]{0:T(256)} %copy-done.136) | copy-start | bytes 2368
  461.7 4.1 collective-permute-start.3
  481.7 20.3 %all-to-all-start.10 = ((bf16[32,19,384]{2,1,0:T(8,128)(2,1)}), bf16[32,19,384]{2,1,0:T(8,128)(2,1)}, u32[]{:S(2)}, u32[]{:S(2)}) async-start(bf16[32,19,384]{2,1,0:T(8,128)(2,1)} %reshape.2440), calls=%async_computation.10 | async-start | bytes 1179648 | tf_op jit(solution)/shard_map/all_to_all | solution.py:175
  520.8 19.6 %all-to-all-start.11 = ((bf16[32,19,384]{2,1,0:T(8,128)(2,1)}), bf16[32,19,384]{2,1,0:T(8,128)(2,1)}, u32[]{:S(2)}, u32[]{:S(2)}) async-start(bf16[32,19,384]{2,1,0:T(8,128)(2,1)} %reshape_transpose_reshape.29), calls=%async_computation.11 | async-start | bytes 1179648 | tf_op jit(solution)/shard_map/all_to_all | solution.py:189
  525.4 391.6 %all-reduce.11.cloned.1.call-start = ((), (), s32[]{:S(2)}) async-start(), calls=%async_computation.13 | async-start | bytes 4718592 | tf_op jit(solution)/shard_map/psum | solution.py:284
  530.2 11.3 %copy-start.141 = (s32[1024]{0:T(1024)S(1)}, s32[1024]{0:T(1024)}, u32[]{:S(2)}) copy-start(s32[1024]{0:T(1024)} %pad_clamp_fusion) | copy-start | bytes 12292
  532.6 16.2 %copy-start.97 = (f32[197]{0:T(256)S(1)}, f32[197]{0:T(256)}, u32[]{:S(2)}) copy-start(f32[197]{0:T(256)} %copy-done.96) | copy-start | bytes 2368
  532.7 388.9 %all-reduce.9.cloned.1.call-start = ((), (), s32[]{:S(2)}) async-start(), calls=%async_computation.12 | async-start | bytes 4718592 | tf_op jit(solution)/shard_map/psum | solution.py:279
  544.1 10.1 %copy-start.9 = (bf16[1,384,384]{2,1,0:T(8,128)(2,1)S(1)}, bf16[1,384,384]{2,1,0:T(8,128)(2,1)}, u32[]{:S(2)}) copy-start(bf16[1,384,384]{2,1,0:T(8,128)(2,1)} %param.15) | copy-start | bytes 884740
  544.1 13.6 %copy-start.99 = (f32[6,197]{1,0:T(8,128)S(1)}, f32[6,197]{1,0:T(8,128)}, u32[]{:S(2)}) copy-start(f32[6,197]{1,0:T(8,128)} %get-tuple-element.104) | copy-start | bytes 14188
  (128 other events, 471.6 us)
Sparse Core Ops, SparseCore 0:
  532.8 78.1 all-reduce.10
  617.3 134.9 all-reduce.8
where the time goes:
time: 946 us; the launch traced here: 933 us
  blocking collectives  344 us (36%)
  matrix products  157 us (17%)
  local copies, waits for them, and re-layouts  146 us (15%)
  other arithmetic  98.3 us (10%)
  waiting for transfers between devices  95.9 us (10%)
  starting transfers between devices  74.7 us (8%)
  between operations  17.1 us (2%)
    psum x1, blocking collectives, body(): lax.psum((dense_total[0], dense_total[1], dense_total[2], dense_total[3],...  344 us
    dot_general x3, matrix products, block_backward(): jnp.einsum('erd,efd->erf', d_produced, w_back, preferred_element_type=jnp...  34.8 us
    dot_general x3, matrix products, block_forward(): jnp.einsum('erd,edf->erf', inputs, w_in, preferred_element_type=jnp.float32)  31.1 us
    all_to_all x3, waiting for transfers between devices, block_forward(): lax.all_to_all(from_experts(produced, arrived.shape[0] // local, capacity...  30.9 us
    all_to_all x3, waiting for transfers between devices, block_forward(): lax.all_to_all(filled.reshape(experts, capacity, width), 'expert', split_...  26.4 us
    all_to_all x3, waiting for transfers between devices, block_backward(): lax.all_to_all(from_experts(d_inputs, sources, capacity), 'expert', split...  24.3 us
    all_to_all x3, starting transfers between devices, block_forward(): lax.all_to_all(filled.reshape(experts, capacity, width), 'expert', split_...  20.9 us
    all_to_all x3, starting transfers between devices, block_backward(): lax.all_to_all(from_experts(d_inputs, sources, capacity), 'expert', split...  19.4 us
  transfers between devices with their start and end apart: 18, of which 11 were waited for; matrix products, arithmetic and copies ran while one was open for 16% of the time, Pallas kernels for 0%

commit v1 on v0

v1 whole, which is shorter than its diff:
```python
import math

import jax
import jax.numpy as jnp
from jax import lax
from jax.experimental import pallas as pl
from jax.experimental.pallas import tpu as pltpu
from jax.sharding import PartitionSpec as P

HEADS = 6
HEAD = 64
PAIR = 2 * HEAD
SCALE = HEAD ** (-0.5)
EPSILON = 1e-06
HIGHEST = lax.Precision.HIGHEST
BF = jnp.bfloat16
F32 = jnp.float32
LANE = 128
MAIN = 16
TAIL = 4
KP = 256
CHUNK = 256
MESH = pl.DeviceIdType.MESH


def mm(a, b, precision=None):
    return lax.dot_general(a, b, (((1,), (0,)), ((), ())), precision=precision, preferred_element_type=F32)


def mm_nt(a, b, precision=None):
    return lax.dot_general(a, b, (((1,), (1,)), ((), ())), precision=precision, preferred_element_type=F32)


def mm_tn(a, b, precision=None):
    return lax.dot_general(a, b, (((0,), (0,)), ((), ())), precision=precision, preferred_element_type=F32)


def iota(shape, dim):
    return lax.broadcasted_iota(jnp.int32, shape, dim)


def one_hot(hit, dtype=BF):
    return jnp.where(hit, 1.0, 0.0).astype(dtype)


def gelu_parts(h):
    z = jnp.abs(h) * (0.5**0.5)
    t = 1.0 / (1.0 + 0.3275911 * z)
    ex = jnp.exp(-(z * z))
    poly = t * (0.127414796 + t * (-0.142248368 + t * (0.7107068705 + t * (-0.7265760135 + t * 0.5307027145))))
    q = poly * ex
    phi = jnp.where(h >= 0.0, 1.0 - q, q)
    return h * phi, phi + h * (ex * (1.0 / math.sqrt(2.0 * math.pi)))


def norm_parts(x):
    cen = x - jnp.mean(x, axis=-1, keepdims=True)
    rstd = lax.rsqrt(jnp.mean(cen * cen, axis=-1, keepdims=True) + EPSILON)
    return cen * rstd, rstd


def norm_back(d_hat, hat, rstd):
    return rstd * (
        d_hat
        - jnp.mean(d_hat, axis=-1, keepdims=True)
        - hat * jnp.mean(d_hat * hat, axis=-1, keepdims=True)
    )


def kernel(dims, *refs):
    seq, width, ff, ne = dims
    t_rows = -(-seq // 16) * 16
    rm, rt = ne * MAIN, ne * TAIL
    rows = rm + rt
    bits = ne.bit_length() - 1
    (
        images, cot, meta, small, w_qkv, w_out, w_in, w_back,
        act_o, ig_o, dense_o, sm_o, wi_o, wi2_o, wb_o, wb2_o,
        meta_s, small_s, wqkv_s, wout_s, win_s, wback_s,
        st_s, s_s, xh1, rs1, xh2, rs2, nrm, qs, ps, att, mix, sec, sec_f, prb, cols_s, gate_s, pk, dd, dt,
        tx, rx, in_s, ac_s, dg_s, dh_s, dp_s, ret, acc, vs, dsr, dbr, dqkv, dmx, ya, ya_rx, gx, gx_rx,
        wtx_i, wtx_b, wrc_i, wrc_b, wrd_i, wrd_b,
        den, den_rc, smt, sm_rc, rs_rx, smrs_rx, dpt, dpr, smdpt, smdpr, agt, ag_rx, smag, smag_rx, dfin, smfin,
        wsem, wsend, a2s, a2r, cxs, cxr, dps, dpr_sem, rss, rsr, ags, agr, acs, acr, igs, igr, osem,
    ) = refs
    core = lax.axis_index("section")
    me = lax.axis_index("expert")
    half = lax.axis_index("dp")
    other = 1 - core

    def expert_at(k):
        return lax.rem(me + k, ne)

    def wait(ref, sem):
        pltpu.make_async_copy(ref, ref, sem).wait()

    def to_core(src, dst, send, recv):
        return pltpu.make_async_remote_copy(
            src_ref=src, dst_ref=dst, send_sem=send, recv_sem=recv,
            device_id={"section": other}, device_id_type=MESH,
        )

    def to_dp(src, dst, send, recv):
        return pltpu.make_async_remote_copy(
            src_ref=src, dst_ref=dst, send_sem=send, recv_sem=recv,
            device_id={"dp": 1 - half}, device_id_type=MESH,
        )

    barrier = pltpu.get_barrier_semaphore()

    def greet(k, _):
        pl.semaphore_signal(barrier, inc=1, device_id={"expert": expert_at(k)}, device_id_type=MESH)
        return _

    lax.fori_loop(1, ne, greet, 0)
    pl.semaphore_signal(barrier, inc=1, device_id={"section": other}, device_id_type=MESH)
    pl.semaphore_signal(barrier, inc=1, device_id={"dp": 1 - half}, device_id_type=MESH)

    held = [
        (meta.at[core], meta.at[other], meta_s),
        (small, small, small_s),
        (w_qkv.at[0], w_qkv.at[0], wqkv_s),
        (w_out.at[0], w_out.at[0], wout_s),
        (w_in.at[0, 0], w_in.at[0, 0], win_s),
        (w_back.at[0, 0], w_back.at[0, 0], wback_s),
    ]
    for i, (mine, _, dst) in enumerate(held):
        pltpu.make_async_copy(mine, dst.at[core], wsem.at[core, i]).start()

    for ref in (nrm, qs, att, sec):
        for b in range(2):
            ref[b, t_rows:KP, :] = jnp.zeros((KP - t_rows, ref.shape[2]), BF)
    for ref in (dbr, dqkv):
        ref[t_rows:KP, :] = jnp.zeros((KP - t_rows, ref.shape[1]), BF)
    for b in range(2):
        vs[b, t_rows:KP, :] = jnp.zeros((KP - t_rows, width), BF)
    smt[...] = jnp.zeros(smt.shape, F32)
    row, col = iota((rm, 3 * rt), 0), iota((rm, 3 * rt), 1)
    chunk = (col >= rt).astype(jnp.int32) + (col >= 2 * rt).astype(jnp.int32)
    n = col - chunk * rt
    st_s[...] = one_hot(((row >> 4) == (n & (ne - 1))) & ((row & 15) == 4 * chunk + (n >> bits)))
    row, col = iota((3 * rt, rm), 0), iota((3 * rt, rm), 1)
    chunk = (row >= rt).astype(jnp.int32) + (row >= 2 * rt).astype(jnp.int32)
    n = row - chunk * rt
    s_s[...] = one_hot(((col >> 4) == (n & (ne - 1))) & ((col & 15) == 4 * chunk + (n >> bits)))

    def padded(value):
        gx[0, t_rows - 16:t_rows, :] = jnp.zeros((16, width), F32)
        gx[0, 0:seq, :] = value.astype(F32)
        return gx[0, 0:t_rows, :]

    pl.semaphore_wait(barrier, ne + 1)
    for i, (_, theirs, dst) in enumerate(held):
        to_core(theirs, dst.at[core], wsend.at[i], wsem.at[core, i]).start()

    def weight(b, i):
        wait(held[i][2].at[b], wsem.at[b, i])

    def pack(phase, main, tail):
        for c in range(3):
            tx[phase, :, 16 * c:16 * c + 16, :] = main[:, LANE * c:LANE * c + LANE].reshape(ne, 16, LANE)
        stack = jnp.concatenate([tail[:, LANE * c:LANE * c + LANE] for c in range(3)], axis=0)
        tx[phase, :, 48:64, :] = mm(st_s[...], stack).astype(BF).reshape(ne, 16, LANE)

    def unpack(phase, out):
        for c in range(3):
            out[0:rm, LANE * c:LANE * c + LANE] = rx[phase, :, 16 * c:16 * c + 16, :].reshape(rm, LANE)
        tail = mm(s_s[...], rx[phase, :, 48:64, :].reshape(rm, LANE)).astype(BF)
        for c in range(3):
            out[rm:rows, LANE * c:LANE * c + LANE] = tail[c * rt:c * rt + rt]

    def exchange(phase):
        def step(k, _):
            pltpu.make_async_remote_copy(
                src_ref=tx.at[phase, k], dst_ref=rx.at[phase, ne - k],
                send_sem=a2s.at[phase], recv_sem=a2r.at[phase],
                device_id={"expert": expert_at(k)}, device_id_type=MESH,
            ).start()
            return _

        lax.fori_loop(1, ne, step, 0)
        rx[phase, 0] = tx[phase, 0]

    def arrived(phase):
        wait(rx.at[phase, pl.ds(1, ne - 1)], a2r.at[phase])

    def place_of(rank, slot):
        return jnp.where(slot < MAIN, rank * MAIN + slot, rm + (slot - MAIN) * ne + rank)

    def route(b):
        data = meta_s[b]
        mef = me.astype(F32)
        chosen, keeps = [data[0:1], data[1:2]], [data[2:3], data[3:4]]
        rank = [r - mef for r in chosen]
        rank = [jnp.where(r < 0.0, r + ne, r) for r in rank]
        lanes = iota((ne, KP), 0).astype(F32)
        marks = [one_hot(lanes == r, F32) for r in rank]
        earlier = one_hot(iota((KP, KP), 0) < iota((KP, KP), 1))
        before = mm((marks[0] + marks[1]).astype(BF), earlier)
        slot = [jnp.sum(before * m, axis=0, keepdims=True) for m in marks]
        spot = iota((rows, KP), 0).astype(F32)
        for k in range(2):
            dt[b, :, KP * k:KP * k + KP] = one_hot(spot == place_of(rank[k], slot[k]))
        which = iota((8, KP), 0)
        lines = jnp.zeros((8, KP), F32)
        for i, line in enumerate((*rank, *slot, *keeps, *chosen)):
            lines = jnp.where(which == i, line, lines)
        same = one_hot(iota((t_rows, KP), 0) == iota((t_rows, KP), 1))
        cols = mm_nt(same, lines.astype(BF))
        cols_s[b] = cols
        spot = iota((t_rows, rows), 1).astype(F32)
        for k in range(2):
            dd[b, k] = one_hot(spot == place_of(cols[:, k:k + 1], cols[:, 2 + k:3 + k]))

    def chosen_marks(b):
        lanes = iota((t_rows, ne), 1).astype(F32)
        return [one_hot(lanes == cols_s[b, :, 6 + k:7 + k], F32) * cols_s[b, :, 4 + k:5 + k] for k in range(2)]

    def head_masks():
        lanes = iota((1, PAIR), 1)
        return [one_hot(lanes < HEAD), one_hot(lanes >= HEAD)]

    def forward_dense(b, x):
        hat, rstd = norm_parts(x)
        xh1[b], rs1[b] = hat, rstd
        normed = (hat * small_s[b, ne:ne + 1, :]).astype(BF)
        nrm[b, 0:t_rows, :] = normed
        weight(b, 2)
        qs[b, 0:t_rows, :] = mm(normed, wqkv_s[b]).astype(BF)
        masks = head_masks()
        real = iota((t_rows, KP), 1) < seq
        for p in range(HEADS // 2):
            at = PAIR * p
            query, key = qs[b, 0:t_rows, at:at + PAIR], qs[b, :, width + at:width + at + PAIR]
            value = qs[b, :, 2 * width + at:2 * width + at + PAIR]
            out = jnp.zeros((t_rows, PAIR), F32)
            for h in range(2):
                scores = mm_nt(query * masks[h], key) * SCALE
                scores = jnp.where(real, scores, -1e30)
                e = jnp.exp(scores - jnp.max(scores, axis=-1, keepdims=True))
                probs = e * (1.0 / jnp.sum(e, axis=-1, keepdims=True))
                ps[b, 2 * p + h] = probs
                out = out + mm(probs.astype(BF), value * masks[h])
            att[b, 0:t_rows, at:at + PAIR] = out.astype(BF)
        weight(b, 3)
        mixed = x + mm(att[b, 0:t_rows, :], wout_s[b])
        mix[b] = mixed
        hat, rstd = norm_parts(mixed)
        xh2[b], rs2[b] = hat, rstd
        second = hat * small_s[b, ne + 1:ne + 2, :]
        sec_f[b] = second
        sec[b, 0:t_rows, :] = second.astype(BF)
        spread = dt[b, :, 0:KP] + dt[b, :, KP:2 * KP]
        pack(4 * b, mm(spread[0:rm], sec[b]).astype(BF), mm(spread[rm:rows], sec[b]).astype(BF))
        exchange(4 * b)
        logits = mm_nt(second, small_s[b, 0:ne, :], HIGHEST)
        e = jnp.exp(logits - jnp.max(logits, axis=-1, keepdims=True))
        probs = e / jnp.sum(e, axis=-1, keepdims=True)
        prb[b] = probs
        for k, marks in enumerate(chosen_marks(b)):
            gate_s[b, k] = jnp.sum(marks * probs, axis=-1, keepdims=True)

    def forward_expert(b):
        weight(b, 4)
        weight(b, 5)
        arrived(4 * b)
        unpack(4 * b, in_s.at[b])
        acc[...] = jnp.zeros(acc.shape, F32)

        def step(i, _):
            at = pl.ds(pl.multiple_of(i * CHUNK, CHUNK), CHUNK)
            active, slope = gelu_parts(mm(in_s[b], win_s[b, :, at]))
            active = active.astype(BF)
            ac_s[b, :, at] = active
            dg_s[b, :, at] = slope.astype(BF)
            acc[...] += mm(active, wback_s[b, at, :])
            return _

        lax.fori_loop(0, ff // CHUNK, step, 0)
        pack(4 * b + 1, acc[0:rm, :].astype(BF), acc[rm:rows, :].astype(BF))
        exchange(4 * b + 1)

    def forward_combine(b):
        arrived(4 * b + 1)
        unpack(4 * b + 1, ret)
        y = mix[b]
        for k in range(2):
            picked = mm(dd[b, k], ret[...])
            pk[b, k] = picked.astype(BF)
            y = y + gate_s[b, k] * picked
        low = y.astype(BF)
        ya[b] = low
        return low.astype(F32)

    def backward_start(b, dy):
        d_probs = jnp.zeros((t_rows, ne), F32)
        for k, marks in enumerate(chosen_marks(b)):
            d_gate = jnp.sum(dy * pk[b, k].astype(F32), axis=-1, keepdims=True)
            d_probs = d_probs + marks * d_gate
            vs[k, 0:t_rows, :] = (gate_s[b, k] * dy).astype(BF)
        stacked = vs[...].reshape(2 * KP, width)
        pack(4 * b + 2, mm(dt[b, 0:rm], stacked).astype(BF), mm(dt[b, rm:rows], stacked).astype(BF))
        exchange(4 * b + 2)
        probs = prb[b]
        d_logits = probs * (d_probs - jnp.sum(probs * d_probs, axis=-1, keepdims=True))
        dsr[...] = mm(d_logits, small_s[b, 0:ne, :], HIGHEST)
        return mm_tn(d_logits, sec_f[b], HIGHEST)

    def backward_expert(b):
        arrived(4 * b + 2)
        unpack(4 * b + 2, dp_s)
        acc[...] = jnp.zeros(acc.shape, F32)

        def step(i, _):
            at = pl.ds(pl.multiple_of(i * CHUNK, CHUNK), CHUNK)
            d_hidden = (mm_nt(dp_s[...], wback_s[b, at, :]) * dg_s[b, :, at].astype(F32)).astype(BF)
            dh_s[:, at] = d_hidden
            acc[...] += mm_nt(d_hidden, win_s[b, :, at])
            return _

        lax.fori_loop(0, ff // CHUNK, step, 0)
        pack(4 * b + 3, acc[0:rm, :].astype(BF), acc[rm:rows, :].astype(BF))
        exchange(4 * b + 3)

    def expert_grads(b):
        def step(i, _):
            at = pl.ds(pl.multiple_of(i * CHUNK, CHUNK), CHUNK)
            wtx_i[:, at] = mm_tn(in_s[b], dh_s[:, at]).astype(BF)
            wtx_b[at, :] = mm_tn(ac_s[b, :, at], dp_s[...]).astype(BF)
            return _

        lax.fori_loop(0, ff // CHUNK, step, 0)

        @pl.when(core != b)
        def _():
            to_core(wtx_i, wrc_i, cxs.at[0], cxr.at[0]).start()
            to_core(wtx_b, wrc_b, cxs.at[1], cxr.at[1]).start()

        @pl.when(core == b)
        def _():
            wait(wrc_i, cxr.at[0])
            wtx_i[...] = (wtx_i[...].astype(F32) + wrc_i[...].astype(F32)).astype(BF)
            to_dp(wtx_i, wrd_i, dps.at[0], dpr_sem.at[0]).start()
            pltpu.make_async_copy(wtx_i, wi_o, osem.at[0]).start()
            wait(wrc_b, cxr.at[1])
            wtx_b[...] = (wtx_b[...].astype(F32) + wrc_b[...].astype(F32)).astype(BF)
            to_dp(wtx_b, wrd_b, dps.at[1], dpr_sem.at[1]).start()
            pltpu.make_async_copy(wtx_b, wb_o, osem.at[1]).start()

    def grads_sent(b):
        @pl.when(core != b)
        def _():
            wait(wtx_i, cxs.at[0])
            wait(wtx_b, cxs.at[1])
            wait(den, cxs.at[2])
            wait(smt, cxs.at[3])

        @pl.when(core == b)
        def _():
            wait(wtx_i, dps.at[0])
            wait(wtx_b, dps.at[1])
            wait(wi_o, osem.at[0])
            wait(wb_o, osem.at[1])

    def backward_dense(b, dy, d_router):
        arrived(4 * b + 3)
        unpack(4 * b + 3, ret)
        d_second = mm(dd[b, 0] + dd[b, 1], ret[...]) + dsr[...]
        hat2 = xh2[b]
        d_gain_two = jnp.sum(d_second * hat2, axis=0, keepdims=True)
        d_mixed = dy + norm_back(d_second * small_s[b, ne + 1:ne + 2, :], hat2, rs2[b])
        dmx[...] = d_mixed
        d_branch = d_mixed.astype(BF)
        dbr[0:t_rows, :] = d_branch
        piece = width * 4 // ne
        per = ne // 4
        den[3 * per:4 * per] = mm_tn(att[b], dbr[...]).astype(BF).reshape(per, piece, width)
        d_att = mm_nt(d_branch, wout_s[b]).astype(BF)
        masks = head_masks()
        for p in range(HEADS // 2):
            at = PAIR * p
            query, key = qs[b, 0:t_rows, at:at + PAIR], qs[b, :, width + at:width + at + PAIR]
            value = qs[b, :, 2 * width + at:2 * width + at + PAIR]
            d_query = jnp.zeros((t_rows, PAIR), F32)
            d_key = jnp.zeros((KP, PAIR), F32)
            d_value = jnp.zeros((KP, PAIR), F32)
            for h in range(2):
                d_out = d_att[:, at:at + PAIR] * masks[h]
                probs = ps[b, 2 * p + h]
                d_value = d_value + mm_tn(probs.astype(BF), d_out)
                d_probs = mm_nt(d_out, value)
                inner = jnp.sum(probs * d_probs, axis=-1, keepdims=True)
                d_scores = (probs * (d_probs - inner)).astype(BF)
                d_query = d_query + mm(d_scores, key * masks[h])
                d_key = d_key + mm_tn(d_scores, query * masks[h])
            dqkv[0:t_rows, at:at + PAIR] = (d_query * SCALE).astype(BF)
            dqkv[:, width + at:width + at + PAIR] = (d_key * SCALE).astype(BF)
            dqkv[:, 2 * width + at:2 * width + at + PAIR] = d_value.astype(BF)
        d_normed = mm_nt(dqkv[0:t_rows, :], wqkv_s[b])
        hat1 = xh1[b]
        d_gain_one = jnp.sum(d_normed * hat1, axis=0, keepdims=True)
        d_x = dmx[...] + norm_back(d_normed * small_s[b, ne:ne + 1, :], hat1, rs1[b])
        for q in range(3):
            grad = mm_tn(nrm[b], dqkv[:, width * q:width * q + width])
            den[q * per:q * per + per] = grad.astype(BF).reshape(per, piece, width)
        for c in range(3):
            at = LANE * c
            smt[:, c, :] = d_router[:, at:at + LANE]
            smt[c, 3:4, :] = d_gain_one[:, at:at + LANE]
            smt[c, 4:5, :] = d_gain_two[:, at:at + LANE]

        @pl.when(core != b)
        def _():
            to_core(den, den_rc, cxs.at[2], cxr.at[2]).start()
            to_core(smt, sm_rc, cxs.at[3], cxr.at[3]).start()

        return d_x

    def dense_scatter(b):
        @pl.when(core == b)
        def _():
            wait(den_rc, cxr.at[2])
            den[...] = (den[...].astype(F32) + den_rc[...].astype(F32)).astype(BF)
            wait(sm_rc, cxr.at[3])
            smt[...] = smt[...] + sm_rc[...]

            def step(k, _):
                to = expert_at(k)
                pltpu.make_async_remote_copy(
                    src_ref=den.at[to], dst_ref=rs_rx.at[ne - k], send_sem=rss.at[0], recv_sem=rsr.at[0],
                    device_id={"expert": to}, device_id_type=MESH,
                ).start()
                pltpu.make_async_remote_copy(
                    src_ref=smt.at[to], dst_ref=smrs_rx.at[ne - k], send_sem=rss.at[1], recv_sem=rsr.at[1],
                    device_id={"expert": to}, device_id_type=MESH,
                ).start()
                return _

            lax.fori_loop(1, ne, step, 0)

    def dense_reduce(b):
        @pl.when(core == b)
        def _():
            peers = pl.ds(1, ne - 1)
            wait(rs_rx.at[peers], rsr.at[0])
            wait(smrs_rx.at[peers], rsr.at[1])
            dpt[...] = den[me].astype(F32)
            smdpt[...] = smt[me]

            def step(k, _):
                dpt[...] += rs_rx[k].astype(F32)
                smdpt[...] += smrs_rx[k]
                return _

            lax.fori_loop(1, ne, step, 0)
            to_dp(dpt, dpr, dps.at[2], dpr_sem.at[2]).start()
            to_dp(smdpt, smdpr, dps.at[3], dpr_sem.at[3]).start()
            wait(rs_rx.at[peers], rss.at[0])
            wait(smrs_rx.at[peers], rss.at[1])

    def dense_gather(b):
        @pl.when(core == b)
        def _():
            wait(dpr, dpr_sem.at[2])
            wait(smdpr, dpr_sem.at[3])
            agt[...] = (dpt[...] + dpr[...]).astype(BF)
            smag[...] = smdpt[...] + smdpr[...]

            def step(k, _):
                to = expert_at(k)
                pltpu.make_async_remote_copy(
                    src_ref=agt, dst_ref=ag_rx.at[ne - k], send_sem=ags.at[0], recv_sem=agr.at[0],
                    device_id={"expert": to}, device_id_type=MESH,
                ).start()
                pltpu.make_async_remote_copy(
                    src_ref=smag, dst_ref=smag_rx.at[ne - k], send_sem=ags.at[1], recv_sem=agr.at[1],
                    device_id={"expert": to}, device_id_type=MESH,
                ).start()
                return _

            lax.fori_loop(1, ne, step, 0)
            dfin[me] = agt[...]
            smfin[me] = smag[...]

    def dense_finish(b):
        @pl.when(core == b)
        def _():
            peers = pl.ds(1, ne - 1)
            wait(ag_rx.at[peers], agr.at[0])
            wait(smag_rx.at[peers], agr.at[1])

            def step(k, _):
                dfin[expert_at(k)] = ag_rx[k]
                smfin[expert_at(k)] = smag_rx[k]
                return _

            lax.fori_loop(1, ne, step, 0)
            pltpu.make_async_copy(dfin, dense_o, osem.at[2]).start()
            pltpu.make_async_copy(smfin, sm_o, osem.at[3]).start()
            wait(ag_rx.at[peers], ags.at[0])
            wait(smag_rx.at[peers], ags.at[1])
            wait(dpt, dps.at[2])
            wait(smdpt, dps.at[3])

    for b in range(2):
        weight(b, 0)
        weight(b, 1)
        route(b)
        if b == 0:
            x = padded(images[core, 0])
        forward_dense(b, x)
        forward_expert(b)
        x = forward_combine(b)
    to_core(ya.at[other], ya_rx, acs, acr).start()
    dy = padded(cot[core, 0])
    dmx[...] = dy
    dy = dmx[...]
    for b in (1, 0):
        d_router = backward_start(b, dy)
        if b == 0:
            dense_reduce(1)
        backward_expert(b)
        if b == 0:
            dense_gather(1)
            grads_sent(1)
        expert_grads(b)
        dx = backward_dense(b, dy, d_router)
        if b == 1:
            dy = dx.astype(BF).astype(F32)
            gx[1] = dy
            dense_scatter(1)
        else:
            gx[0] = dx
    to_core(gx.at[other], gx_rx, igs, igr).start()
    dense_scatter(0)
    dense_finish(1)
    dense_reduce(0)
    dense_gather(0)
    wait(ya_rx, acr)
    pltpu.make_async_copy(ya.at[core], act_o.at[core], osem.at[4]).start()
    pltpu.make_async_copy(ya_rx, act_o.at[other], osem.at[5]).start()
    wait(gx_rx, igr)
    pltpu.make_async_copy(gx.at[core], ig_o.at[core], osem.at[6]).start()
    pltpu.make_async_copy(gx_rx, ig_o.at[other], osem.at[7]).start()
    wait(wrd_i, dpr_sem.at[0])
    pltpu.make_async_copy(wrd_i, wi2_o, osem.at[8]).start()
    wait(wrd_b, dpr_sem.at[1])
    pltpu.make_async_copy(wrd_b, wb2_o, osem.at[9]).start()
    dense_finish(0)
    grads_sent(0)
    for i, (_, theirs, _dst) in enumerate(held):
        wait(theirs, wsend.at[i])
    for phase in range(8):
        wait(tx.at[phase, pl.ds(1, ne - 1)], a2s.at[phase])
    wait(ya.at[other], acs)
    wait(gx.at[other], igs)
    for i, ref in enumerate((dense_o, sm_o, act_o.at[0], act_o.at[0], ig_o.at[0], ig_o.at[0], wi2_o, wb2_o)):
        wait(ref, osem.at[2 + i])


def body(images_in, cotangent, gain_one, w_qkv, w_out, gain_two, w_router, w_in, w_back, routes, keep):
    micro, _, seq, width = images_in.shape
    ne = lax.axis_size("expert")
    ff = w_in.shape[3]
    t_rows = -(-seq // 16) * 16
    rm, rt = ne * MAIN, ne * TAIL
    rows = rm + rt
    piece = 4 * width // ne
    pad = ((0, 0), (0, 0), (0, KP - seq))
    chosen = jnp.pad(jnp.swapaxes(routes[0, :, 0], 1, 2).astype(F32), pad, constant_values=-64.0)
    kept = jnp.pad(jnp.swapaxes(keep[0, :, 0], 1, 2).astype(F32), pad)
    meta = jnp.concatenate([chosen, kept, jnp.zeros((micro, 4, KP), F32)], axis=1)
    small = jnp.concatenate([w_router[0].T, gain_one, gain_two, jnp.zeros((6, width), F32)], axis=0)
    vmem, anywhere = pl.BlockSpec(memory_space=pltpu.VMEM), pl.BlockSpec(memory_space=pl.ANY)
    dma = pltpu.SemaphoreType.DMA

    def v(*shape, dtype=BF):
        return pltpu.VMEM(shape, dtype)

    t, r, w = t_rows, rows, width
    scratch = [
        v(2, 8, KP, dtype=F32), v(2, ne + 8, w, dtype=F32),
        v(2, w, 3 * w), v(2, w, w), v(2, w, ff), v(2, ff, w),
        v(rm, 3 * rt), v(3 * rt, rm),
        v(2, t, w, dtype=F32), v(2, t, 1, dtype=F32), v(2, t, w, dtype=F32), v(2, t, 1, dtype=F32),
        v(2, KP, w), v(2, KP, 3 * w), v(2, HEADS, t, KP, dtype=F32), v(2, KP, w),
        v(2, t, w, dtype=F32), v(2, KP, w), v(2, t, w, dtype=F32), v(2, t, ne, dtype=F32),
        v(2, t, 8, dtype=F32), v(2, 2, t, 1, dtype=F32), v(2, 2, t, w), v(2, 2, t, r), v(2, r, 2 * KP),
        v(8, ne, 64, LANE), v(8, ne, 64, LANE), v(2, r, w), v(2, r, ff), v(2, r, ff), v(r, ff), v(r, w), v(r, w),
        v(r, w, dtype=F32), v(2, KP, w), v(t, w, dtype=F32), v(KP, w), v(KP, 3 * w), v(t, w, dtype=F32),
        v(2, t, w), v(t, w), v(2, t, w, dtype=F32), v(t, w, dtype=F32),
        v(w, ff), v(ff, w), v(w, ff), v(ff, w), v(w, ff), v(ff, w),
        v(ne, piece, w), v(ne, piece, w), v(ne, 8, LANE, dtype=F32), v(ne, 8, LANE, dtype=F32),
        v(ne, piece, w), v(ne, 8, LANE, dtype=F32),
        v(piece, w, dtype=F32), v(piece, w, dtype=F32), v(8, LANE, dtype=F32), v(8, LANE, dtype=F32),
        v(piece, w), v(ne, piece, w), v(8, LANE, dtype=F32), v(ne, 8, LANE, dtype=F32),
        v(ne, piece, w), v(ne, 8, LANE, dtype=F32),
        dma((2, 6)), dma((6,)), dma((8,)), dma((8,)), dma((4,)), dma((4,)), dma((4,)), dma((4,)),
        dma((2,)), dma((2,)), dma((2,)), dma((2,)), dma, dma, dma, dma, dma((10,)),
    ]
    shapes = [
        ((2, t, w), BF), ((2, t, w), F32), ((ne, piece, w), BF), ((ne, 8, LANE), F32),
        ((w, ff), BF), ((w, ff), BF), ((ff, w), BF), ((ff, w), BF),
    ]
    act, grad, dense, sm, wi, wi2, wb, wb2 = pl.pallas_call(
        lambda *refs: kernel((seq, width, ff, ne), *refs),
        out_shape=[jax.ShapeDtypeStruct(s, d) for s, d in shapes],
        in_specs=[vmem] * 4 + [anywhere] * 4,
        out_specs=[anywhere] * 8,
        scratch_shapes=scratch,
        compiler_params=pltpu.CompilerParams(
            collective_id=0, has_side_effects=True, vmem_limit_bytes=62 * 2**20
        ),
        name="blocks",
    )(images_in, cotangent, meta, small, w_qkv, w_out, w_in, w_back)
    dense = dense.reshape(4, width, width).astype(F32)
    d_w_qkv = jnp.concatenate([dense[0], dense[1], dense[2]], axis=1)
    d_router = sm[:, 0:3].reshape(ne, width).T
    return (
        act[None, :, None, :seq],
        grad[None, :, None, :seq],
        sm[0:3, 3].reshape(1, width),
        d_w_qkv[None],
        dense[3][None],
        sm[0:3, 4].reshape(1, width),
        d_router[None],
        (wi.astype(F32) + wi2.astype(F32))[None, None],
        (wb.astype(F32) + wb2.astype(F32))[None, None],
    )


def solution(mesh):
    spread = ("expert", "dp")
    tokens = P(None, spread, None, None)
    per_block = P("section", None, spread, None, None)
    vector, matrix, experts = P("section", None), P("section", None, None), P("section", "expert", None, None)
    return jax.shard_map(
        body,
        mesh=mesh,
        in_specs=(
            tokens, tokens, vector, matrix, matrix, vector, matrix, experts, experts, per_block, per_block,
        ),
        out_specs=(
            per_block, per_block, vector, matrix, matrix, vector, matrix, experts, experts,
        ),
        check_vma=False,
    )
```

time: 946 us -> 230 us (0.24); the launches traced: 933 us -> 229 us
  blocking collectives: 344 us -> 0 us
  Pallas kernels: 0 us -> 209 us
  matrix products: 157 us -> 0 us
  local copies, waits for them, and re-layouts: 146 us -> 11.7 us
  waiting for transfers between devices: 95.9 us -> 0 us
  other arithmetic: 98.3 us -> 7.61 us
  starting transfers between devices: 74.7 us -> 0 us
  between operations: 17.1 us -> 0.71 us
    psum x1 -> x0, blocking collectives: 344 us -> none  [body(): lax.psum((dense_total[0], dense_total[1], dense_total[2], dense_total[3],...]
    pallas_call x0 -> x1, Pallas kernels: none -> 209 us  [body(): pl.pallas_call(lambda *refs: kernel((seq, width, ff, ne), *refs), out_sha...]
    dot_general x69 -> x0, matrix products: 157 us -> none  [the longest x3 34.8 us: block_backward(): jnp.einsum('erd,efd->erf', d_produced, w_back, preferred_element_type=jnp...]
    all_to_all x12 -> x0, waiting for transfers between devices: 95.9 us -> none  [the longest x3 30.9 us: block_forward(): lax.all_to_all(from_experts(produced, arrived.shape[0] // local, capacity...]
    all_to_all x12 -> x0, starting transfers between devices: 67.7 us -> none  [the longest x3 20.9 us: block_forward(): lax.all_to_all(filled.reshape(experts, capacity, width), 'expert', split_...]
    reduce_sum x48 -> x0, other arithmetic: 38.3 us -> none  [the longest x14 10.8 us: layer_norm(): center = values - jnp.mean(values, axis=-1, keepdims=True)]
    reshape x15 -> x0, local copies, waits for them, and re-layouts: 21 us -> none  [the longest x3 4.96 us: block_backward(): d_returned.reshape(experts, capacity, width)]
    another operation x17 -> x1, local copies, waits for them, and re-layouts: 19.3 us -> 1.35 us  [body(): sm[0:3, 4].reshape(1, width)]
  transfers between devices with their start and end apart: 18 -> 0, of which waited for: 11 -> 0; matrix products, arithmetic and copies ran while one was open for 16% -> 0% of each run, Pallas kernels for 0% -> 0%
where the time goes in v1:
time: 230 us; the launch traced here: 229 us
  Pallas kernels  209 us (91%)
  local copies, waits for them, and re-layouts  11.7 us (5%)
  other arithmetic  7.61 us (3%)
    pallas_call x1, Pallas kernels, body(): pl.pallas_call(lambda *refs: kernel((seq, width, ff, ne), *refs), out_sha...  209 us
    unnamed x17, local copies, waits for them, and re-layouts  7.2 us

profile of v1, /device:TPU:0, one launch (start us, length us, event | category | flops | bytes accessed | tf_op | source)
XLA Modules:
  0.0 229.2 jit_solution(683866934216416666)
XLA Ops:
  0.7 0.1 pad.19.clone
  0.7 0.1 pad.16.clone
  0.8 0.7 fusion.2
  1.5 0.7 fusion.refs_2_
  2.2 1.5 maximum_maximum_fusion.refs_3_
  3.7 1.7 copy.28.refs_0_
  5.4 1.7 copy.29.refs_1_
  7.2 209.1 %blocks.1 = (bf16[2,208,384]{2,1,0:T(8,128)(2,1)}, f32[2,208,384]{2,1,0:T(8,128)}, bf16[32,48,384]{2,1,0:T(8,128)(2,1)}, f32[32,8,128]{2,1,0:T(8,128)}, bf16[384...) custom-call(bf16[2,1,197,384]{3,2,1,0:T(8,128)(2,1)} %copy.28.refs_0_, ...), custom_call_target="tpu_custom_call" | custom-call | tf_op jit(solution)/shard_map/blocks/pallas_call | solution.py:605
  216.3 0.0 copy-start.5
  216.3 1.1 slice_bitcast_fusion.1
  217.4 0.0 copy-start.3
  217.4 0.0 copy-start.4
  217.4 1.0 copy.30
  218.4 1.4 slice_bitcast_fusion.2
  219.7 0.9 slice.42
  220.6 0.6 copy.34
  221.3 0.0 copy-done.5
  221.3 1.4 copy.31
  222.7 0.0 copy-done.3
  222.7 0.0 copy-done.4
  222.7 0.0 copy-start.1
  222.7 0.0 copy-start.2
  222.8 1.7 add_bitcast_fusion.1
  224.5 0.0 copy-done.1
  224.5 0.7 copy-done.2
  225.2 0.0 copy-start
  225.2 1.6 add_bitcast_fusion
  226.9 0.0 copy-done
  226.9 1.0 fusion.4
  227.9 1.3 maximum_bitcast_fusion
  (3 shorter events, 0.0 us)
Async XLA Ops:
  216.3 4.9 %copy-start.5 = (f32[2,208,384]{2,1,0:T(8,128)S(1)}, f32[2,208,384]{2,1,0:T(8,128)}, u32[]{:S(2)}) copy-start(f32[2,208,384]{2,1,0:T(8,128)} %get-tuple-element.18) | copy-start | bytes 1916932
  217.4 5.4 %copy-start.3 = (bf16[384,1536]{1,0:T(8,128)(2,1)S(1)}, bf16[384,1536]{1,0:T(8,128)(2,1)}, u32[]{:S(2)}) copy-start(bf16[384,1536]{1,0:T(8,128)(2,1)} %get-tuple-element.21) | copy-start | bytes 3538948
  217.4 5.3 %copy-start.4 = (bf16[384,1536]{1,0:T(8,128)(2,1)S(1)}, bf16[384,1536]{1,0:T(8,128)(2,1)}, u32[]{:S(2)}) copy-start(bf16[384,1536]{1,0:T(8,128)(2,1)} %get-tuple-element.22) | copy-start | bytes 3538948
  222.7 1.8 copy-start.1
  222.7 2.5 %copy-start.2 = (bf16[1536,384]{1,0:T(8,128)(2,1)S(1)}, bf16[1536,384]{1,0:T(8,128)(2,1)}, u32[]{:S(2)}) copy-start(bf16[1536,384]{1,0:T(8,128)(2,1)} %get-tuple-element.24) | copy-start | bytes 3538948
  225.2 1.6 copy-start

commit v2 on v1

v2 whole, which is shorter than its diff:
```python
import math

import jax
import jax.numpy as jnp
from jax import lax
from jax.experimental import pallas as pl
from jax.experimental.pallas import tpu as pltpu
from jax.sharding import PartitionSpec as P

HEADS = 6
HEAD = 64
PAIR = 2 * HEAD
SCALE = HEAD ** (-0.5)
EPSILON = 1e-06
HIGHEST = lax.Precision.HIGHEST
BF = jnp.bfloat16
F32 = jnp.float32
LANE = 128
MAIN = 16
TAIL = 4
KP = 256
CHUNK = 512
ORDER = (0, 1, 4, 5, 6, 7, 2, 3)
GROUPS = 4
MESH = pl.DeviceIdType.MESH


def mm(a, b, precision=None):
    return lax.dot_general(a, b, (((1,), (0,)), ((), ())), precision=precision, preferred_element_type=F32)


def mm_nt(a, b, precision=None):
    return lax.dot_general(a, b, (((1,), (1,)), ((), ())), precision=precision, preferred_element_type=F32)


def mm_tn(a, b, precision=None):
    return lax.dot_general(a, b, (((0,), (0,)), ((), ())), precision=precision, preferred_element_type=F32)


def iota(shape, dim):
    return lax.broadcasted_iota(jnp.int32, shape, dim)


def one_hot(hit, dtype=BF):
    return jnp.where(hit, 1.0, 0.0).astype(dtype)


def phi_of(h):
    return 0.5 * lax.erf(h * (0.5**0.5)) + 0.5


def slope_of(h, phi):
    return phi + h * (jnp.exp(h * h * -0.5) * (1.0 / math.sqrt(2.0 * math.pi)))


def norm_parts(x):
    cen = x - jnp.mean(x, axis=-1, keepdims=True)
    rstd = lax.rsqrt(jnp.mean(cen * cen, axis=-1, keepdims=True) + EPSILON)
    return cen * rstd, rstd


def norm_back(d_hat, hat, rstd):
    return rstd * (
        d_hat
        - jnp.mean(d_hat, axis=-1, keepdims=True)
        - hat * jnp.mean(d_hat * hat, axis=-1, keepdims=True)
    )


def kernel(dims, *refs):
    seq, width, ff, ne = dims
    t_rows = -(-seq // 16) * 16
    gs = ne // GROUPS
    gm, gt = gs * MAIN, gs * TAIL
    gr = gm + gt
    rows = ne * (MAIN + TAIL)
    piece = width * 4 // ne
    per = ne // 4
    (
        images, cot, routes, keep, gain_one, gain_two, router, w_qkv, w_out, w_in, w_back,
        act_o, ig_o, qkv_o, out_o, sm_o, wi_o, wb_o,
        meta_m, meta_s, small_m, small_s, wqkv_s, wout_s, win_s, wback_s,
        s_s, xh1, rs1, xh2, rs2, nrm, qs, ps, att, mix, sec, prb, cols_s, gate_s, pk, dd, dt,
        tx, rx, in_s, ac_s, dg_s, dp_s, ret, vs, dsr, dbr, dqkv, dmx, ya, ya_rx, gx, gx_rx,
        wtx_i, wtx_b, wrc_i, wrc_b,
        den, den_rc, smt, rs_rx, dpt, dpr, agt, ag_rx, dfin_q, smfin,
        wsem, wsend, a2s, a2r, cxs, cxr, dps, dpr_sem, rss, rsr, ags, agr, acs, acr, igs, igr, osem,
    ) = refs
    core = lax.axis_index("section")
    me = lax.axis_index("expert")
    half = lax.axis_index("dp")
    other = 1 - core

    def expert_at(k):
        return lax.rem(me + k, ne)

    def wait(ref, sem):
        pltpu.make_async_copy(ref, ref, sem).wait()

    def to_core(src, dst, send, recv):
        return pltpu.make_async_remote_copy(
            src_ref=src, dst_ref=dst, send_sem=send, recv_sem=recv,
            device_id={"section": other}, device_id_type=MESH,
        )

    def to_dp(src, dst, send, recv):
        return pltpu.make_async_remote_copy(
            src_ref=src, dst_ref=dst, send_sem=send, recv_sem=recv,
            device_id={"dp": 1 - half}, device_id_type=MESH,
        )

    barrier = pltpu.get_barrier_semaphore()

    def greet(k, _):
        pl.semaphore_signal(barrier, inc=1, device_id={"expert": expert_at(k)}, device_id_type=MESH)
        return _

    pl.semaphore_signal(barrier, inc=1, device_id={"section": other}, device_id_type=MESH)
    pl.semaphore_signal(barrier, inc=1, device_id={"dp": 1 - half}, device_id_type=MESH)
    lax.fori_loop(1, ne, greet, 0)

    which = iota((8, KP), 0)
    for m in range(2):
        meta_m[m] = jnp.where(which < 2, -64.0, 0.0)
        meta_m[m, 0:2, 0:seq] = routes[m].astype(F32)
        meta_m[m, 2:4, 0:seq] = keep[m].astype(F32)
    small_m[0:ne] = router[...]
    small_m[ne:ne + 1] = gain_one[...]
    small_m[ne + 1:ne + 2] = gain_two[...]
    small_m[ne + 2:ne + 8] = jnp.zeros((6, width), F32)
    held = [
        (meta_m.at[core], meta_m.at[other], meta_s),
        (small_m, small_m, small_s),
        (w_qkv.at[0], w_qkv.at[0], wqkv_s),
        (w_out.at[0], w_out.at[0], wout_s),
        (w_in.at[0, 0], w_in.at[0, 0], win_s),
        (w_back.at[0, 0], w_back.at[0, 0], wback_s),
    ]
    for i, (mine, _, dst) in enumerate(held):
        pltpu.make_async_copy(mine, dst.at[core], wsem.at[core, i]).start()

    for ref in (nrm, qs, att, sec):
        for b in range(2):
            ref[b, t_rows:KP, :] = jnp.zeros((KP - t_rows, ref.shape[2]), BF)
    for ref in (dbr, dqkv):
        ref[t_rows:KP, :] = jnp.zeros((KP - t_rows, ref.shape[1]), BF)
    for b in range(2):
        vs[b, t_rows:KP, :] = jnp.zeros((KP - t_rows, width), BF)
    smt[...] = jnp.zeros(smt.shape, F32)
    row, col = iota((3 * gt, gm), 0), iota((3 * gt, gm), 1)
    chunk = (row >= gt).astype(jnp.int32) + (row >= 2 * gt).astype(jnp.int32)
    n = row - chunk * gt
    bits = gs.bit_length() - 1
    s_s[...] = one_hot(((col >> 4) == (n & (gs - 1))) & ((col & 15) == 4 * chunk + (n >> bits)))

    pl.semaphore_wait(barrier, ne + 1)
    for i, (_, theirs, dst) in enumerate(held):
        to_core(theirs, dst.at[core], wsend.at[i], wsem.at[core, i]).start()

    def weight(b, i):
        wait(held[i][2].at[b], wsem.at[b, i])

    def send(phase, g, rows_of, back):
        main, tail = rows_of[0:gm], rows_of[gm:gr]
        at = pl.ds(g * gs, gs)
        slot = ORDER.index(phase) % 4
        if g == (GROUPS - 1 if back else 0) and ORDER.index(phase) >= 4:
            wait(tx.at[slot, pl.ds(1, ne - 1)], a2s.at[slot])
        for c in range(3):
            tx[slot, at, 16 * c:16 * c + 16, :] = main[:, LANE * c:LANE * c + LANE].reshape(gs, 16, LANE)
        stack = jnp.concatenate([tail[:, LANE * c:LANE * c + LANE] for c in range(3)], axis=0)
        tx[slot, at, 48:64, :] = mm_tn(s_s[...], stack).astype(BF).reshape(gs, 16, LANE)
        own = 0 if back else ne - 1
        first = 1 if back and g == 0 else g * gs
        last = ne - 1 if not back and g == GROUPS - 1 else g * gs + gs

        def step(i, _):
            pltpu.make_async_remote_copy(
                src_ref=tx.at[slot, i], dst_ref=rx.at[phase, ne - 1 - i],
                send_sem=a2s.at[slot], recv_sem=a2r.at[phase, GROUPS - 1 - g],
                device_id={"expert": expert_at(i if back else i + 1)}, device_id_type=MESH,
            ).start()
            return _

        lax.fori_loop(first, last, step, 0)
        if g * gs <= own < g * gs + gs:
            pltpu.make_async_copy(
                tx.at[slot, own], rx.at[phase, ne - 1 - own], a2r.at[phase, GROUPS - 1 - g]
            ).start()

    def receive(phase, g, out, start):
        at = pl.ds(g * gs, gs)
        wait(rx.at[phase, at], a2r.at[phase, g])
        for c in range(3):
            out[start:start + gm, LANE * c:LANE * c + LANE] = rx[phase, at, 16 * c:16 * c + 16, :].reshape(gm, LANE)
        tail = mm(s_s[...], rx[phase, at, 48:64, :].reshape(gm, LANE)).astype(BF)
        for c in range(3):
            out[start + gm:start + gr, LANE * c:LANE * c + LANE] = tail[c * gt:c * gt + gt]

    def place_of(rank, slot):
        group = jnp.floor(rank * (1.0 / gs))
        within = rank - group * gs
        return group * gr + jnp.where(slot < MAIN, within * MAIN + slot, gm + (slot - MAIN) * gs + within)

    def route(b):
        data = meta_s[b]
        mef = (me + 1).astype(F32)
        chosen, keeps = [data[0:1], data[1:2]], [data[2:3], data[3:4]]
        rank = [r - mef for r in chosen]
        rank = [jnp.where(r < 0.0, r + ne, r) for r in rank]
        lanes = iota((ne, KP), 0).astype(F32)
        marks = [one_hot(lanes == r, F32) for r in rank]
        earlier = one_hot(iota((KP, KP), 0) < iota((KP, KP), 1))
        before = mm((marks[0] + marks[1]).astype(BF), earlier)
        slot = [jnp.sum(before * m, axis=0, keepdims=True) for m in marks]
        spot = iota((rows, KP), 0).astype(F32)
        for k in range(2):
            dt[b, :, KP * k:KP * k + KP] = one_hot(spot == place_of(rank[k], slot[k]))
        which = iota((8, KP), 0)
        lines = jnp.zeros((8, KP), F32)
        for i, line in enumerate((*rank, *slot, *keeps, *chosen)):
            lines = jnp.where(which == i, line, lines)
        same = one_hot(iota((t_rows, KP), 0) == iota((t_rows, KP), 1))
        cols = mm_nt(same, lines.astype(BF))
        cols_s[b] = cols
        spot = iota((t_rows, rows), 1).astype(F32)
        for k in range(2):
            dd[b, k] = one_hot(spot == place_of(cols[:, k:k + 1], cols[:, 2 + k:3 + k]))

    def chosen_marks(b):
        lanes = iota((t_rows, ne), 1).astype(F32)
        return [one_hot(lanes == cols_s[b, :, 6 + k:7 + k], F32) * cols_s[b, :, 4 + k:5 + k] for k in range(2)]

    def head_masks():
        lanes = iota((1, PAIR), 1)
        return [one_hot(lanes < HEAD), one_hot(lanes >= HEAD)]

    def forward_dense(b, x):
        hat, rstd = norm_parts(x)
        xh1[b], rs1[b] = hat, rstd
        normed = (hat * small_s[b, ne:ne + 1, :]).astype(BF)
        nrm[b, 0:t_rows, :] = normed
        weight(b, 2)
        qs[b, 0:t_rows, :] = mm(normed, wqkv_s[b]).astype(BF)
        masks = head_masks()
        real = iota((t_rows, KP), 1) < seq
        for p in range(HEADS // 2):
            at = PAIR * p
            query, key = qs[b, 0:t_rows, at:at + PAIR], qs[b, :, width + at:width + at + PAIR]
            value = qs[b, :, 2 * width + at:2 * width + at + PAIR]
            out = jnp.zeros((t_rows, PAIR), F32)
            for h in range(2):
                scores = mm_nt(query * masks[h], key) * SCALE
                scores = jnp.where(real, scores, -1e30)
                e = jnp.exp(scores - jnp.max(scores, axis=-1, keepdims=True))
                probs = e * (1.0 / jnp.sum(e, axis=-1, keepdims=True))
                ps[b, 2 * p + h] = probs
                out = out + mm(probs.astype(BF), value * masks[h])
            att[b, 0:t_rows, at:at + PAIR] = out.astype(BF)
        weight(b, 3)
        mixed = x + mm(att[b, 0:t_rows, :], wout_s[b])
        mix[...] = mixed
        hat, rstd = norm_parts(mixed)
        xh2[b], rs2[b] = hat, rstd
        second = hat * small_s[b, ne + 1:ne + 2, :]
        sec[b, 0:t_rows, :] = second.astype(BF)
        for g in range(GROUPS):
            at = slice(g * gr, g * gr + gr)
            send(4 * b, g, mm(dt[b, at, 0:KP] + dt[b, at, KP:2 * KP], sec[b]).astype(BF), False)
        logits = mm_nt(second, small_s[b, 0:ne, :], HIGHEST)
        e = jnp.exp(logits - jnp.max(logits, axis=-1, keepdims=True))
        probs = e / jnp.sum(e, axis=-1, keepdims=True)
        prb[b] = probs
        for k, marks in enumerate(chosen_marks(b)):
            gate_s[b, k] = jnp.sum(marks * probs, axis=-1, keepdims=True)

    steps = ff // CHUNK

    def chunk_at(i):
        return pl.ds(pl.multiple_of(i * CHUNK, CHUNK), CHUNK)

    def forward_expert(b):
        weight(b, 4)
        weight(b, 5)
        for h in range(GROUPS - 1, -1, -1):
            at = slice(h * gr, h * gr + gr)
            receive(4 * b, h, in_s.at[b, 0], h * gr)
            hidden = mm(in_s[b, 0, at, :], win_s[b])
            active = (hidden * phi_of(hidden)).astype(BF)
            ac_s[b, 0, at, :] = active
            send(4 * b + 1, h, mm(active, wback_s[b]).astype(BF), True)

    def slopes(b, side):
        def step(n, _):
            at = pl.ds(pl.multiple_of(lax.rem(n, GROUPS) * gr, 16), gr)
            cols = chunk_at(lax.div(n, GROUPS))
            hidden = mm(in_s[b, side, at, :], win_s[b, :, cols])
            phi = phi_of(hidden)
            dg_s[b, side, at, cols] = slope_of(hidden, phi).astype(BF)
            if side == 1:
                ac_s[b, side, at, cols] = (hidden * phi).astype(BF)
            return _

        lax.fori_loop(0, GROUPS * steps, step, 0)

    def rows_to_dp(ref, b, i):
        to_dp(ref.at[b, 0], ref.at[b, 1], dps.at[i], dpr_sem.at[i]).start()

    def rows_from_dp(ref, b, i):
        wait(ref.at[b, 1], dpr_sem.at[i])

    def forward_combine(b):
        for g in range(GROUPS):
            receive(4 * b + 1, g, ret, g * gr)
        rows_to_dp(in_s, b, b)
        y = mix[...]
        for k in range(2):
            picked = mm(dd[b, k], ret[...])
            pk[b, k] = picked.astype(BF)
            y = y + gate_s[b, k] * picked
        low = y.astype(BF)
        ya[b] = low
        return low.astype(F32)

    def backward_start(b, dy):
        d_probs = jnp.zeros((t_rows, ne), F32)
        for k, marks in enumerate(chosen_marks(b)):
            d_gate = jnp.sum(dy * pk[b, k].astype(F32), axis=-1, keepdims=True)
            d_probs = d_probs + marks * d_gate
            vs[k, 0:t_rows, :] = (gate_s[b, k] * dy).astype(BF)
        for g in range(GROUPS):
            at = slice(g * gr, g * gr + gr)
            part = mm(dt[b, at, 0:KP], vs[0]) + mm(dt[b, at, KP:2 * KP], vs[1])
            send(4 * b + 2, g, part.astype(BF), False)
        probs = prb[b]
        d_logits = probs * (d_probs - jnp.sum(probs * d_probs, axis=-1, keepdims=True))
        dsr[...] = mm(d_logits, small_s[b, 0:ne, :], HIGHEST)
        return mm_tn(d_logits, xh2[b] * small_s[b, ne + 1:ne + 2, :], HIGHEST)

    def hidden_grad(b, side, at, cols):
        slope = dg_s[b, side, at, cols].astype(F32)
        d_hidden = (mm_nt(dp_s[b, side, at, :], wback_s[b, cols, :]) * slope).astype(BF)
        dg_s[b, side, at, cols] = d_hidden
        return d_hidden

    def backward_expert(b):
        for h in range(GROUPS - 1, -1, -1):
            at = slice(h * gr, h * gr + gr)
            receive(4 * b + 2, h, dp_s.at[b, 0], h * gr)
            d_hidden = hidden_grad(b, 0, at, slice(None))
            send(4 * b + 3, h, mm_nt(d_hidden, win_s[b]).astype(BF), True)

    def far_hidden_grad(b):
        rows_from_dp(dp_s, b, 2 + b)

        def step(n, _):
            hidden_grad(b, 1, pl.ds(pl.multiple_of(lax.rem(n, GROUPS) * gr, 16), gr), chunk_at(lax.div(n, GROUPS)))
            return _

        lax.fori_loop(0, GROUPS * steps, step, 0)

    def in_grads(b):
        def step(i, _):
            cols = chunk_at(i)
            grad = mm_tn(in_s[b].reshape(2 * rows, width), dg_s[b, :, :, cols].reshape(2 * rows, CHUNK))
            wtx_i[:, cols] = grad.astype(BF)
            return _

        lax.fori_loop(0, steps, step, 0)

        @pl.when(core != b)
        def _():
            to_core(wtx_i, wrc_i, cxs.at[0], cxr.at[0]).start()

    def back_grads(b):
        def step(i, _):
            cols = chunk_at(i)
            grad = mm_tn(ac_s[b, :, :, cols].reshape(2 * rows, CHUNK), dp_s[b].reshape(2 * rows, width))
            wtx_b[cols, :] = grad.astype(BF)
            return _

        lax.fori_loop(0, steps, step, 0)

        @pl.when(core != b)
        def _():
            to_core(wtx_b, wrc_b, cxs.at[1], cxr.at[1]).start()

    def expert_out(b):
        @pl.when(core == b)
        def _():
            wait(wrc_i, cxr.at[0])
            wtx_i[...] = (wtx_i[...].astype(F32) + wrc_i[...].astype(F32)).astype(BF)
            pltpu.make_async_copy(wtx_i, wi_o, osem.at[0]).start()
            wait(wrc_b, cxr.at[1])
            wtx_b[...] = (wtx_b[...].astype(F32) + wrc_b[...].astype(F32)).astype(BF)
            pltpu.make_async_copy(wtx_b, wb_o, osem.at[1]).start()

    def in_sent(b):
        @pl.when(core != b)
        def _():
            wait(wtx_i, cxs.at[0])

        @pl.when(core == b)
        def _():
            wait(wi_o, osem.at[0])

    def back_sent(b):
        @pl.when(core != b)
        def _():
            wait(wtx_b, cxs.at[1])

        @pl.when(core == b)
        def _():
            wait(wb_o, osem.at[1])

    def dense_sent(b):
        @pl.when(core != b)
        def _():
            wait(den, cxs.at[2])

        @pl.when(core == b)
        def _():
            wait(den.at[pl.ds(1, ne - 1)], rss)

    def keep_dense(q, grad):
        for c in range(3):
            part = grad[:, LANE * c:LANE * c + LANE].astype(BF)
            den[q * per:q * per + per, piece * c:piece * c + piece, :] = part.reshape(per, piece, LANE)

    def backward_attention(b, dy):
        for g in range(GROUPS):
            receive(4 * b + 3, g, ret, g * gr)
        rows_to_dp(dp_s, b, 2 + b)
        d_second = mm(dd[b, 0] + dd[b, 1], ret[...]) + dsr[...]
        hat2 = xh2[b]
        d_gain_two = jnp.sum(d_second * hat2, axis=0, keepdims=True)
        d_mixed = dy + norm_back(d_second * small_s[b, ne + 1:ne + 2, :], hat2, rs2[b])
        dmx[...] = d_mixed
        d_branch = d_mixed.astype(BF)
        dbr[0:t_rows, :] = d_branch
        d_att = mm_nt(d_branch, wout_s[b]).astype(BF)
        masks = head_masks()
        for p in range(HEADS // 2):
            at = PAIR * p
            query, key = qs[b, 0:t_rows, at:at + PAIR], qs[b, :, width + at:width + at + PAIR]
            value = qs[b, :, 2 * width + at:2 * width + at + PAIR]
            d_query = jnp.zeros((t_rows, PAIR), F32)
            d_key = jnp.zeros((KP, PAIR), F32)
            d_value = jnp.zeros((KP, PAIR), F32)
            for h in range(2):
                d_out = d_att[:, at:at + PAIR] * masks[h]
                probs = ps[b, 2 * p + h]
                d_value = d_value + mm_tn(probs.astype(BF), d_out)
                d_probs = mm_nt(d_out, value)
                inner = jnp.sum(probs * d_probs, axis=-1, keepdims=True)
                d_scores = (probs * (d_probs - inner)).astype(BF)
                d_query = d_query + mm(d_scores, key * masks[h])
                d_key = d_key + mm_tn(d_scores, query * masks[h])
            dqkv[0:t_rows, at:at + PAIR] = (d_query * SCALE).astype(BF)
            dqkv[:, width + at:width + at + PAIR] = (d_key * SCALE).astype(BF)
            dqkv[:, 2 * width + at:2 * width + at + PAIR] = d_value.astype(BF)
        return d_gain_two

    def backward_input(b):
        d_normed = mm_nt(dqkv[0:t_rows, :], wqkv_s[b])
        hat1 = xh1[b]
        d_gain_one = jnp.sum(d_normed * hat1, axis=0, keepdims=True)
        return dmx[...] + norm_back(d_normed * small_s[b, ne:ne + 1, :], hat1, rs1[b]), d_gain_one

    def dense_grads(b):
        keep_dense(3, mm_tn(att[b], dbr[...]))
        for q in range(3):
            keep_dense(q, mm_tn(nrm[b], dqkv[:, width * q:width * q + width]))

    def dense_send(b, d_router, d_gain_one, d_gain_two):
        for c in range(3):
            at = LANE * c
            smt[:, c, :] = d_router[:, at:at + LANE]
            smt[c, 3:4, :] = d_gain_one[:, at:at + LANE]
            smt[c, 4:5, :] = d_gain_two[:, at:at + LANE]
        den[:, 3 * piece:3 * piece + 16, :] = smt[...].astype(BF)

        @pl.when(core != b)
        def _():
            to_core(den, den_rc, cxs.at[2], cxr.at[2]).start()

    def dense_scatter(b):
        @pl.when(core == b)
        def _():
            wait(den_rc, cxr.at[2])

            def step(k, _):
                to = expert_at(k)
                den[to] = (den[to].astype(F32) + den_rc[to].astype(F32)).astype(BF)
                pltpu.make_async_remote_copy(
                    src_ref=den.at[to], dst_ref=rs_rx.at[ne - k], send_sem=rss, recv_sem=rsr,
                    device_id={"expert": to}, device_id_type=MESH,
                ).start()
                return _

            lax.fori_loop(1, ne, step, 0)
            dpt[...] = den[me].astype(F32) + den_rc[me].astype(F32)

    def dense_reduce(b):
        @pl.when(core == b)
        def _():
            wait(rs_rx.at[pl.ds(1, ne - 1)], rsr)

            def step(k, total):
                return total + rs_rx[k].astype(F32)

            dpt[...] = lax.fori_loop(1, ne, step, dpt[...])
            to_dp(dpt, dpr, dps.at[4], dpr_sem.at[4]).start()

    def dense_gather(b):
        @pl.when(core == b)
        def _():
            wait(dpr, dpr_sem.at[4])
            agt[...] = (dpt[...] + dpr[...]).astype(BF)

            def step(k, _):
                to = expert_at(k)
                pltpu.make_async_remote_copy(
                    src_ref=agt, dst_ref=ag_rx.at[ne - k], send_sem=ags, recv_sem=agr,
                    device_id={"expert": to}, device_id_type=MESH,
                ).start()
                return _

            lax.fori_loop(1, ne, step, 0)

    def dense_finish(b):
        @pl.when(core == b)
        def _():
            wait(ag_rx.at[pl.ds(1, ne - 1)], agr)
            ag_rx[0] = agt[...]

            def step(k, _):
                to = expert_at(k)
                smfin[to] = ag_rx[k, 3 * piece:3 * piece + 16, :]
                block, at = lax.div(to, per), pl.multiple_of(lax.rem(to, per) * piece, 16)
                for c in range(3):
                    dfin_q[block, pl.ds(at, piece), LANE * c:LANE * c + LANE] = ag_rx[k, piece * c:piece * c + piece, :]
                return _

            lax.fori_loop(0, ne, step, 0)
            for q in range(3):
                pltpu.make_async_copy(dfin_q.at[q], qkv_o.at[:, pl.ds(width * q, width)], osem.at[6 + q]).start()
            pltpu.make_async_copy(dfin_q.at[3], out_o, osem.at[9]).start()
            pltpu.make_async_copy(smfin, sm_o, osem.at[10]).start()
            wait(ag_rx.at[pl.ds(1, ne - 1)], ags)
            wait(dpt, dps.at[4])

    x = images[...].astype(F32)
    weight(0, 0)
    weight(0, 1)
    route(0)
    for b in range(2):
        forward_dense(b, x)
        if b == 0:
            weight(1, 0)
            weight(1, 1)
            route(1)
        else:
            rows_from_dp(in_s, 0, 0)
            slopes(0, 1)
        forward_expert(b)
        slopes(b, 0)
        x = forward_combine(b)
    to_core(ya.at[other], ya_rx, acs, acr).start()
    dy = cot[...].astype(F32)
    d_router = backward_start(1, dy)
    rows_from_dp(in_s, 1, 1)
    slopes(1, 1)
    backward_expert(1)
    d_gain_two = backward_attention(1, dy)
    dx, d_gain_one = backward_input(1)
    dy = dx.astype(BF).astype(F32)
    gx[1] = dy
    d_router_0 = backward_start(0, dy)
    dense_grads(1)
    dense_send(1, d_router, d_gain_one, d_gain_two)
    backward_expert(0)
    dense_scatter(1)
    far_hidden_grad(1)
    in_grads(1)
    d_gain_two = backward_attention(0, dy)
    dense_sent(1)
    dense_grads(0)
    dx, d_gain_one = backward_input(0)
    dense_send(0, d_router_0, d_gain_one, d_gain_two)
    gx[0] = dx
    to_core(gx.at[other], gx_rx, igs, igr).start()
    dense_reduce(1)
    dense_scatter(0)
    back_grads(1)
    expert_out(1)
    dense_gather(1)
    far_hidden_grad(0)
    in_sent(1)
    in_grads(0)
    dense_reduce(0)
    back_sent(1)
    back_grads(0)
    dense_finish(1)
    dense_gather(0)
    wait(ya_rx, acr)
    pltpu.make_async_copy(ya.at[core], act_o.at[core], osem.at[2]).start()
    pltpu.make_async_copy(ya_rx, act_o.at[other], osem.at[3]).start()
    wait(gx_rx, igr)
    pltpu.make_async_copy(gx.at[core], ig_o.at[core], osem.at[4]).start()
    pltpu.make_async_copy(gx_rx, ig_o.at[other], osem.at[5]).start()
    expert_out(0)
    dense_finish(0)
    in_sent(0)
    back_sent(0)
    dense_sent(0)
    for i, (_, theirs, _dst) in enumerate(held):
        wait(theirs, wsend.at[i])
    for slot in range(4):
        wait(tx.at[slot, pl.ds(1, ne - 1)], a2s.at[slot])
    for b in range(2):
        wait(in_s.at[b, 0], dps.at[b])
        wait(dp_s.at[b, 0], dps.at[2 + b])
    wait(ya.at[other], acs)
    wait(gx.at[other], igs)
    for i, ref in enumerate((act_o.at[0], act_o.at[0], ig_o.at[0], ig_o.at[0])):
        wait(ref, osem.at[2 + i])
    for q in range(3):
        wait(dfin_q.at[q], osem.at[6 + q])
    wait(out_o, osem.at[9])
    wait(sm_o, osem.at[10])


def body(images_in, cotangent, gain_one, w_qkv, w_out, gain_two, w_router, w_in, w_back, routes, keep):
    micro, _, seq, width = images_in.shape
    ne = lax.axis_size("expert")
    ff = w_in.shape[3]
    t_rows = -(-seq // 16) * 16
    rows = ne * (MAIN + TAIL)
    gs = ne // GROUPS
    piece = 4 * width // ne
    core = lax.axis_index("section")

    def own(tokens):
        mine = lax.dynamic_index_in_dim(tokens[:, 0], core, 0, keepdims=False)
        return jnp.pad(mine, ((0, t_rows - seq), (0, 0)))

    vmem, anywhere = pl.BlockSpec(memory_space=pltpu.VMEM), pl.BlockSpec(memory_space=pl.ANY)
    dma = pltpu.SemaphoreType.DMA

    def v(*shape, dtype=BF):
        return pltpu.VMEM(shape, dtype)

    t, r, w, deep = t_rows, rows, width, 3 * piece + 16
    scratch = [
        v(2, 8, KP, dtype=F32), v(2, 8, KP, dtype=F32), v(ne + 8, w, dtype=F32), v(2, ne + 8, w, dtype=F32),
        v(2, w, 3 * w), v(2, w, w), v(2, w, ff), v(2, ff, w),
        v(3 * gs * TAIL, gs * MAIN),
        v(2, t, w, dtype=F32), v(2, t, 1, dtype=F32), v(2, t, w, dtype=F32), v(2, t, 1, dtype=F32),
        v(2, KP, w), v(2, KP, 3 * w), v(2, HEADS, t, KP, dtype=F32), v(2, KP, w),
        v(t, w, dtype=F32), v(2, KP, w), v(2, t, ne, dtype=F32),
        v(2, t, 8, dtype=F32), v(2, 2, t, 1, dtype=F32), v(2, 2, t, w), v(2, 2, t, r), v(2, r, 2 * KP),
        v(4, ne, 64, LANE), v(8, ne, 64, LANE), v(2, 2, r, w), v(2, 2, r, ff), v(2, 2, r, ff), v(2, 2, r, w),
        v(r, w),
        v(2, KP, w), v(t, w, dtype=F32), v(KP, w), v(KP, 3 * w), v(t, w, dtype=F32),
        v(2, t, w), v(t, w), v(2, t, w, dtype=F32), v(t, w, dtype=F32),
        v(w, ff), v(ff, w), v(w, ff), v(ff, w),
        v(ne, deep, LANE), v(ne, deep, LANE), v(ne, 16, LANE, dtype=F32), v(ne, deep, LANE),
        v(deep, LANE, dtype=F32), v(deep, LANE, dtype=F32), v(deep, LANE), v(ne, deep, LANE),
        v(4, w, w), v(ne, 16, LANE),
        dma((2, 6)), dma((6,)), dma((4,)), dma((8, GROUPS)), dma((3,)), dma((3,)), dma((5,)), dma((5,)),
        dma, dma, dma, dma, dma, dma, dma, dma, dma((11,)),
    ]
    shapes = [
        ((2, t, w), BF), ((2, t, w), F32), ((w, 3 * w), BF), ((w, w), BF), ((ne, 16, LANE), BF),
        ((w, ff), BF), ((ff, w), BF),
    ]
    act, grad, d_qkv, d_out, sm, d_in, d_back = pl.pallas_call(
        lambda *refs: kernel((seq, width, ff, ne), *refs),
        out_shape=[jax.ShapeDtypeStruct(s, d) for s, d in shapes],
        in_specs=[vmem] * 7 + [anywhere] * 4,
        out_specs=[anywhere] * 7,
        scratch_shapes=scratch,
        compiler_params=pltpu.CompilerParams(
            collective_id=0, has_side_effects=True, vmem_limit_bytes=62 * 2**20
        ),
        name="blocks",
    )(
        own(images_in), own(cotangent),
        jnp.swapaxes(routes[0, :, 0], 1, 2), jnp.swapaxes(keep[0, :, 0], 1, 2),
        gain_one, gain_two, w_router[0].T, w_qkv, w_out, w_in, w_back,
    )
    sm = sm.astype(F32)
    return (
        act[None, :, None, :seq],
        grad[None, :, None, :seq],
        sm[0:3, 3].reshape(1, width),
        d_qkv.astype(F32)[None],
        d_out.astype(F32)[None],
        sm[0:3, 4].reshape(1, width),
        sm[:, 0:3].reshape(ne, width).T[None],
        d_in.astype(F32)[None, None],
        d_back.astype(F32)[None, None],
    )


def solution(mesh):
    spread = ("expert", "dp")
    tokens = P(None, spread, None, None)
    per_block = P("section", None, spread, None, None)
    vector, matrix, experts = P("section", None), P("section", None, None), P("section", "expert", None, None)
    return jax.shard_map(
        body,
        mesh=mesh,
        in_specs=(
            tokens, tokens, vector, matrix, matrix, vector, matrix, experts, experts, per_block, per_block,
        ),
        out_specs=(
            per_block, per_block, vector, matrix, matrix, vector, matrix, experts, experts,
        ),
        check_vma=False,
    )
```

time: 230 us -> 190 us (0.83)
  Pallas kernels: 209 us -> 173 us
  local copies, waits for them, and re-layouts: 11.7 us -> 7.63 us
    pallas_call x1, Pallas kernels: 209 us -> 173 us  [body(): pl.pallas_call(lambda *refs: kernel((seq, width, ff, ne), *refs), out_sha...]
    unnamed x17 -> x15, local copies, waits for them, and re-layouts: 7.2 us -> 3.08 us
    broadcast_in_dim x3 -> x4, other arithmetic: 4.7 us -> 6.79 us  [the longest x1 2.92 us: body(): d_back.astype(F32)[None, None]]
where the time goes in v2:
time: 190 us; the launch traced here: 189 us
  Pallas kernels  173 us (91%)
  other arithmetic  7.72 us (4%)
  local copies, waits for them, and re-layouts  7.63 us (4%)
    pallas_call x1, Pallas kernels, body(): pl.pallas_call(lambda *refs: kernel((seq, width, ff, ne), *refs), out_sha...  173 us

profile of v2, /device:TPU:0, one launch (start us, length us, event | category | flops | bytes accessed | tf_op | source)
XLA Modules:
  0.0 189.4 jit_solution(15465738918337190204)
XLA Ops:
  0.6 1.7 constant_dynamic-slice_fusion
  2.4 0.7 pad.7.refs_0_
  3.1 0.7 pad.8.refs_1_
  3.8 173.4 %blocks.1 = (bf16[2,208,384]{2,1,0:T(8,128)(2,1)}, f32[2,208,384]{2,1,0:T(8,128)}, bf16[384,1152]{1,0:T(8,128)(2,1)}, bf16[384,384]{1,0:T(8,128)(2,1)}, bf16[32,...) custom-call(bf16[208,384]{1,0:T(8,128)(2,1)} %pad.7.refs_0_, ...), custom_call_target="tpu_custom_call" | custom-call | tf_op jit(solution)/shard_map/blocks/pallas_call | solution.py:678
  177.1 0.9 convert_element_type.5
  178.1 0.6 slice_bitcast_fusion.2
  178.6 0.8 slice.22
  179.5 0.6 copy.34
  180.1 0.0 copy-start
  180.1 2.9 %bitcast_convert_fusion = f32[1,1,1536,384]{3,2,1,0:T(8,128)} fusion(bf16[1536,384]{1,0:T(8,128)(2,1)} %get-tuple-element.22), kind=kLoop, calls=%fused_computation | loop fusion | flops 589824 | bytes 3538944 | tf_op jit(solution)/shard_map/broadcast_in_dim | solution.py:703
  183.0 0.0 copy-done
  183.0 0.0 copy-start.1
  183.0 1.7 bitcast_convert_fusion.1
  184.7 0.0 copy-start.2
  184.7 0.0 copy-done.1
  184.7 1.3 bitcast_convert_fusion.2
  186.1 0.0 copy-start.3
  186.1 0.0 copy-done.2
  186.1 0.0 copy-start.4
  186.1 1.4 copy.25
  187.6 0.0 copy-done.3
  187.6 1.0 copy.24
  188.5 0.0 copy-done.4
  188.5 0.9 bitcast_convert_fusion.3
  (4 shorter events, 0.1 us)
Async XLA Ops:
  180.1 2.9 %copy-start = (bf16[384,1536]{1,0:T(8,128)(2,1)S(1)}, bf16[384,1536]{1,0:T(8,128)(2,1)}, u32[]{:S(2)}) copy-start(bf16[384,1536]{1,0:T(8,128)(2,1)} %get-tuple-element.21) | copy-start | bytes 3538948
  183.0 1.7 copy-start.1
  184.7 1.3 copy-start.2
  186.1 1.5 copy-start.3
  186.1 2.5 %copy-start.4 = (bf16[384,384]{1,0:T(8,128)(2,1)S(1)}, bf16[384,384]{1,0:T(8,128)(2,1)}, u32[]{:S(2)}) copy-start(bf16[384,384]{1,0:T(8,128)(2,1)} %get-tuple-element.20) | copy-start | bytes 884740
